TPU v7x, 512 devices: a whole 4x8x8 slice. The times are simulated.
512 devices in a mesh: section: 32 (over z_hi, x, core), dp: 16 (over z_lo, y).
Axes of the slice: x: 4, y: 8, z: 8 (z_hi: 4, z_lo: 2; z = z_hi * 2 + z_lo), core: 2. Of those that a mesh axis runs over, the one named last changes fastest.
Arguments:
- adapter_in: bfloat16 [32, 8192, 64], P('section', 'dp'), may hold values from -0.0625 to 0.0625
- adapter_out: bfloat16 [32, 64, 8192], P('section', None, 'dp'), may hold values from -0.375 to 0.375
- down_state: bfloat16 [32, 256, 8192], P('section', 'dp'), may hold values from -6 to 6
- up_state: bfloat16 [32, 256, 8192], P('section', 'dp'), may hold values from -6 to 6
- down_cot: bfloat16 [32, 256, 8192], P('section', 'dp'), may hold values from -6 to 6
- up_cot: bfloat16 [32, 256, 8192], P('section', 'dp'), may hold values from -6 to 6
- down_stash: bfloat16 [32, 3, 256, 8192], P('section', None, 'dp'), may hold values from -6 to 6
- up_stash: bfloat16 [32, 3, 256, 8192], P('section', None, 'dp'), may hold values from -6 to 6
- entering: bfloat16 [2, 2, 256, 8192], P(None, None, 'dp'), may hold values from -6 to 6
Outputs:
- down_out: bfloat16 [32, 256, 8192], P('section', 'dp')
- up_out: bfloat16 [32, 256, 8192], P('section', 'dp')
- down_back: bfloat16 [32, 256, 8192], P('section', 'dp')
- up_back: bfloat16 [32, 256, 8192], P('section', 'dp')
- grad_in: float32 [32, 8192, 64], P('section', 'dp')
- grad_out: float32 [32, 64, 8192], P('section', None, 'dp')
All inputs are finite; a program needn't handle non-finite values.
Results may differ from a plain program's by a relative error of at most 0.019.
Values may be sent and summed in bfloat16 or wider, within the bound.
No kernel may reach another device: no remote copies, remote signals or barrier semaphores. Data moves between devices by JAX's collectives and lax.ppermute only.
A program may use at most 64 MiB of HBM per device.

v0:
```python
import jax
import jax.numpy as jnp
from jax import lax
from jax.sharding import PartitionSpec as P

TICKS = 3


epsilon = 1e-05


def partner(value, axis, bit):
    mask = 2**bit
    pairs = [(source, source ^ mask) for source in range(lax.axis_size(axis))]
    return lax.ppermute(value, axis, pairs)


def shifted(block, axis, distance):
    devices = range(lax.axis_size(axis))
    route = [(i - distance, i) for i in devices if i - distance in devices]
    return lax.ppermute(block, axis, route)


def pieces(rows, cot, w_in, w_out):
    x_wide = rows.astype(jnp.float32)
    inv_rms = lax.rsqrt(jnp.mean(x_wide * x_wide, axis=-1, keepdims=True) + epsilon)
    normed = x_wide * inv_rms
    normed_low = normed.astype(jnp.bfloat16)
    pre_act = jnp.dot(normed_low, w_in, preferred_element_type=jnp.float32)
    sigma = jax.nn.sigmoid(pre_act)
    hidden = (pre_act * sigma).astype(jnp.bfloat16)
    hidden_grad = lax.dot_general(
        cot, w_out, (((1,), (1,)), ((), ())), preferred_element_type=jnp.float32
    )
    pre_grad = (hidden_grad * sigma * (1.0 + pre_act * (1.0 - sigma))).astype(jnp.bfloat16)
    return (inv_rms, normed, normed_low, hidden, pre_grad)


def forward(rows, w_in, w_out):
    x_wide = rows.astype(jnp.float32)
    inv_rms = lax.rsqrt(jnp.mean(x_wide * x_wide, axis=-1, keepdims=True) + epsilon)
    normed_low = (x_wide * inv_rms).astype(jnp.bfloat16)
    pre_act = jnp.dot(normed_low, w_in, preferred_element_type=jnp.float32)
    hidden = (pre_act * jax.nn.sigmoid(pre_act)).astype(jnp.bfloat16)
    return (x_wide + jnp.dot(hidden, w_out, preferred_element_type=jnp.float32)).astype(
        jnp.bfloat16
    )


def backward(rows, cot, w_in, w_out):
    inv_rms, normed, normed_low, hidden, pre_grad = pieces(rows, cot, w_in, w_out)
    normed_grad = lax.dot_general(
        pre_grad, w_in, (((1,), (1,)), ((), ())), preferred_element_type=jnp.float32
    )
    inner = jnp.mean(normed_grad * normed, axis=-1, keepdims=True)
    grad_rows = (cot.astype(jnp.float32) + inv_rms * (normed_grad - normed * inner)).astype(
        jnp.bfloat16
    )
    term_in = lax.dot_general(
        normed_low, pre_grad, (((0,), (0,)), ((), ())), preferred_element_type=jnp.float32
    )
    term_out = lax.dot_general(
        hidden, cot, (((0,), (0,)), ((), ())), preferred_element_type=jnp.float32
    )
    return (grad_rows, term_in, term_out)


def body(
    adapter_in, adapter_out, down_state, up_state, down_cot, up_cot, down_stash, up_stash, entering
):
    sections = lax.axis_size("section")
    position = lax.axis_index("section")
    at_first = position == 0
    at_last = position == sections - 1
    bit_count = sections.bit_length() - 1
    own_in = adapter_in[0]
    own_out = adapter_out[0]
    weight_bits = list(range(bit_count))
    twin_in, twin_out = (own_in, own_out)
    for bit_index in weight_bits:
        twin_in, twin_out = partner((twin_in, twin_out), "section", bit_index)
    down_in, down_wout, up_in, up_wout = (
        lax.all_gather(own_in, "dp", axis=0, tiled=True),
        lax.all_gather(own_out, "dp", axis=1, tiled=True),
        lax.all_gather(twin_in, "dp", axis=0, tiled=True),
        lax.all_gather(twin_out, "dp", axis=1, tiled=True),
    )
    x_down = down_state[0]
    x_up = up_state[0]
    c_down = down_cot[0]
    c_up = up_cot[0]
    sum_in_down = jnp.zeros(down_in.shape, jnp.float32)
    sum_out_down = jnp.zeros(down_wout.shape, jnp.float32)
    sum_in_up = jnp.zeros(up_in.shape, jnp.float32)
    sum_out_up = jnp.zeros(up_wout.shape, jnp.float32)
    for moment in range(TICKS):
        y_down = forward(x_down, down_in, down_wout)
        y_up = forward(x_up, up_in, up_wout)
        xb_down = jnp.where(at_last, x_down, down_stash[0, moment])
        cb_down = jnp.where(at_last, y_down, c_down)
        xb_up = jnp.where(at_first, x_up, up_stash[0, moment])
        cb_up = jnp.where(at_first, y_up, c_up)
        g_down, term_in, term_out = backward(xb_down, cb_down, down_in, down_wout)
        sum_in_down = sum_in_down + term_in
        sum_out_down = sum_out_down + term_out
        g_up, term_in, term_out = backward(xb_up, cb_up, up_in, up_wout)
        sum_in_up = sum_in_up + term_in
        sum_out_up = sum_out_up + term_out
        if moment + 1 < TICKS:
            from_lower = shifted((y_down, g_up), "section", 1)
            from_higher = shifted((y_up, g_down), "section", -1)
            x_down = jnp.where(at_first, entering[0, moment], from_lower[0])
            c_up = from_lower[1]
            x_up = jnp.where(at_last, entering[1, moment], from_higher[0])
            c_down = from_higher[1]
    shard_in_down, shard_out_down, shard_in_up, shard_out_up = (
        lax.psum_scatter(
            sum_in_down.astype(jnp.bfloat16), "dp", scatter_dimension=0, tiled=True
        ).astype(jnp.float32),
        lax.psum_scatter(
            sum_out_down.astype(jnp.bfloat16), "dp", scatter_dimension=1, tiled=True
        ).astype(jnp.float32),
        lax.psum_scatter(
            sum_in_up.astype(jnp.bfloat16), "dp", scatter_dimension=0, tiled=True
        ).astype(jnp.float32),
        lax.psum_scatter(
            sum_out_up.astype(jnp.bfloat16), "dp", scatter_dimension=1, tiled=True
        ).astype(jnp.float32),
    )
    grad_bits = list(range(bit_count))
    for bit_index in grad_bits:
        shard_in_up, shard_out_up = (
            partner(shard_in_up.astype(jnp.bfloat16), "section", bit_index).astype(
                shard_in_up.dtype
            ),
            partner(shard_out_up.astype(jnp.bfloat16), "section", bit_index).astype(
                shard_out_up.dtype
            ),
        )
    grad_in = shard_in_down + shard_in_up
    grad_out = shard_out_down + shard_out_up
    return (y_down[None], y_up[None], g_down[None], g_up[None], grad_in[None], grad_out[None])


def solution(mesh):
    return jax.shard_map(
        body,
        mesh=mesh,
        in_specs=(
            P("section", "dp", None),
            P("section", None, "dp"),
            P("section", "dp", None),
            P("section", "dp", None),
            P("section", "dp", None),
            P("section", "dp", None),
            P("section", None, "dp", None),
            P("section", None, "dp", None),
            P(None, None, "dp", None),
        ),
        out_specs=(
            P("section", "dp", None),
            P("section", "dp", None),
            P("section", "dp", None),
            P("section", "dp", None),
            P("section", "dp", None),
            P("section", None, "dp"),
        ),
        check_vma=False,
    )
```

profile of v0, /device:TPU:2, one launch (start us, length us, event | category | flops | bytes accessed | tf_op | source)
XLA Modules:
  0.0 691.2 jit_solution(15414040863875391610)
XLA Ops:
  12.1 7.8 %collective-permute-start.8 = (bf16[64,512]{1,0:T(8,128)(2,1)S(1)}, bf16[64,512]{1,0:T(8,128)(2,1)S(1)}, u32[]{:S(2)}, u32[]{:S(2)}) collective-permute-start(bf16[64,512]{1,0:T(8,128)(2,1)S(1)} %collective-permute-done.7), channel_id=1, source_target_pairs={{0,32},{16,48},{32,0},{48,16},{64,96},{80,112},{96,64},{112,80},{1... | collective-permute-start | bytes 196616 | tf_op jit(solution)/shard_map/ppermute | solution.py:15
  24.2 5.7 collective-permute-done.9
  32.0 5.7 collective-permute-done.10
  37.6 6.4 collective-permute-start.11
  44.0 4.3 collective-permute-done.11
  55.4 3.1 collective-permute-done.3
  60.9 5.3 collective-permute-done.4
  69.0 4.6 collective-permute-done.5
  73.6 6.6 collective-permute-start.6
  80.1 3.6 collective-permute-done.6
  87.2 71.2 %all-gather.11.cloned.1.call-done = bf16[1,8192,64]{1,2,0:T(8,128)(2,1)} async-done(((bf16[1,512,64]{1,2,0:T(8,128)(2,1)}), bf16[1,8192,64]{1,2,0:T(8,128)(2,1)}) %all-gather.11.cloned.1.call-update) | async-done | bytes 1048592 | tf_op jit(solution)/shard_map/all_gather | solution.py:83
  158.3 3.4 bitcast_select_fusion.7
  163.8 66.6 %all-gather.9.cloned.1.call-done = bf16[64,8192]{1,0:T(8,128)(2,1)} async-done(((bf16[64,512]{1,0:T(8,128)(2,1)}), bf16[64,8192]{1,0:T(8,128)(2,1)}) %all-gather.9.cloned.1.call-update) | async-done | bytes 1048592 | tf_op jit(solution)/shard_map/all_gather | solution.py:86
  230.4 71.9 %all-gather.7.cloned.1.call-done = bf16[8192,64]{0,1:T(8,128)(2,1)} async-done(((bf16[512,64]{0,1:T(8,128)(2,1)}), bf16[8192,64]{0,1:T(8,128)(2,1)}) %all-gather.7.cloned.1.call-update) | async-done | bytes 1048592 | tf_op jit(solution)/shard_map/all_gather | solution.py:85
  302.4 3.3 bitcast_select_fusion.3
  307.7 4.2 collective-permute-done.12
  318.2 3.5 collective-permute-start.1
  334.2 3.2 collective-permute-start.14
  343.1 3.8 collective-permute-start.15
  363.5 5.3 collective-permute-done.17
  377.0 3.6 convolution_add_fusion.7
  390.6 72.9 %reduce-scatter.7.cloned.1.call-done = bf16[512,64]{0,1:T(8,128)(2,1)} async-done(((bf16[8192,64]{0,1:T(8,128)(2,1)}), bf16[512,64]{0,1:T(8,128)(2,1)}) %reduce-scatter.7.cloned.1.call-update) | async-done | bytes 65552 | tf_op jit(solution)/shard_map/reduce_scatter | solution.py:123
  467.4 69.1 %reduce-scatter.11.cloned.1.call-done = bf16[64,512]{1,0:T(8,128)(2,1)} async-done(((bf16[64,8192]{1,0:T(8,128)(2,1)}), bf16[64,512]{1,0:T(8,128)(2,1)}) %reduce-scatter.11.cloned.1.call-update) | async-done | bytes 65552 | tf_op jit(solution)/shard_map/reduce_scatter | solution.py:126
  543.3 3.6 collective-permute-start.24
  546.9 4.0 collective-permute-start.20
  551.3 3.4 collective-permute-start.25
  554.8 4.6 collective-permute-start.21
  559.4 4.1 collective-permute-start.26
  563.5 5.4 collective-permute-start.22
  569.8 4.4 collective-permute-start.27
  574.1 35.6 %reduce-scatter.5.cloned.1.call-done = bf16[512,64]{0,1:T(8,128)(2,1)} async-done(((bf16[8192,64]{0,1:T(8,128)(2,1)}), bf16[512,64]{0,1:T(8,128)(2,1)}) %reduce-scatter.5.cloned.1.call-update) | async-done | bytes 65552 | tf_op jit(solution)/shard_map/reduce_scatter | solution.py:117
  611.2 71.6 %reduce-scatter.9.cloned.1.call-done = bf16[64,512]{1,0:T(8,128)(2,1)} async-done(((bf16[64,8192]{1,0:T(8,128)(2,1)}), bf16[64,512]{1,0:T(8,128)(2,1)}) %reduce-scatter.9.cloned.1.call-update) | async-done | bytes 65552 | tf_op jit(solution)/shard_map/reduce_scatter | solution.py:120
  (198 shorter events, 104.8 us)
Async XLA Ops:
  7.2 80.0 %all-gather.13.cloned.1.call-start = ((), (), s32[]{:S(2)}) async-start(), calls=%async_computation.11 | async-start | bytes 1114112 | tf_op jit(solution)/shard_map/all_gather | solution.py:84
  7.9 150.4 %all-gather.11.cloned.1.call-start = ((), (), s32[]{:S(2)}) async-start(), calls=%async_computation.10 | async-start | bytes 1114112 | tf_op jit(solution)/shard_map/all_gather | solution.py:83
  8.7 221.8 %all-gather.9.cloned.1.call-start = ((), (), s32[]{:S(2)}) async-start(), calls=%async_computation.5 | async-start | bytes 1114112 | tf_op jit(solution)/shard_map/all_gather | solution.py:86
  12.1 10.2 %collective-permute-start.8 = (bf16[64,512]{1,0:T(8,128)(2,1)S(1)}, bf16[64,512]{1,0:T(8,128)(2,1)S(1)}, u32[]{:S(2)}, u32[]{:S(2)}) collective-permute-start(bf16[64,512]{1,0:T(8,128)(2,1)S(1)} %collective-permute-done.7), channel_id=1, source_target_pairs={{0,32},{16,48},{32,0},{48,16},{64,96},{80,112},{96,64},{112,80},{1... | collective-permute-start | bytes 196616 | tf_op jit(solution)/shard_map/ppermute | solution.py:15
  22.3 7.7 %collective-permute-start.9 = (bf16[64,512]{1,0:T(8,128)(2,1)S(1)}, bf16[64,512]{1,0:T(8,128)(2,1)S(1)}, u32[]{:S(2)}, u32[]{:S(2)}) collective-permute-start(bf16[64,512]{1,0:T(8,128)(2,1)S(1)} %collective-permute-done.8), channel_id=1, source_target_pairs={{0,64},{16,80},{32,96},{48,112},{64,0},{80,16},{96,32},{112,48},{1... | collective-permute-start | bytes 196616 | tf_op jit(solution)/shard_map/ppermute | solution.py:15
  29.9 7.7 %collective-permute-start.10 = (bf16[64,512]{1,0:T(8,128)(2,1)S(1)}, bf16[64,512]{1,0:T(8,128)(2,1)S(1)}, u32[]{:S(2)}, u32[]{:S(2)}) collective-permute-start(bf16[64,512]{1,0:T(8,128)(2,1)S(1)} %collective-permute-done.9), channel_id=1, source_target_pairs={{0,128},{16,144},{32,160},{48,176},{64,192},{80,208},{96,224},{112... | collective-permute-start | bytes 196616 | tf_op jit(solution)/shard_map/ppermute | solution.py:15
  37.6 10.7 %collective-permute-start.11 = (bf16[64,512]{1,0:T(8,128)(2,1)S(1)}, bf16[64,512]{1,0:T(8,128)(2,1)S(1)}, u32[]{:S(2)}, u32[]{:S(2)}) collective-permute-start(bf16[64,512]{1,0:T(8,128)(2,1)S(1)} %collective-permute-done.10), channel_id=1, source_target_pairs={{0,256},{16,272},{32,288},{48,304},{64,320},{80,336},{96,352},{112... | collective-permute-start | bytes 196616 | tf_op jit(solution)/shard_map/ppermute | solution.py:15
  49.0 253.4 %all-gather.7.cloned.1.call-start = ((), (), s32[]{:S(2)}) async-start(), calls=%async_computation.4 | async-start | bytes 1114112 | tf_op jit(solution)/shard_map/all_gather | solution.py:85
  58.5 7.7 %collective-permute-start.4 = (bf16[512,64]{0,1:T(8,128)(2,1)S(1)}, bf16[512,64]{0,1:T(8,128)(2,1)S(1)}, u32[]{:S(2)}, u32[]{:S(2)}) collective-permute-start(bf16[512,64]{0,1:T(8,128)(2,1)S(1)} %collective-permute-done.3), channel_id=1, source_target_pairs={{0,64},{16,80},{32,96},{48,112},{64,0},{80,16},{96,32},{112,48},{1... | collective-permute-start | bytes 196616 | tf_op jit(solution)/shard_map/ppermute | solution.py:15
  66.2 7.4 %collective-permute-start.5 = (bf16[512,64]{0,1:T(8,128)(2,1)S(1)}, bf16[512,64]{0,1:T(8,128)(2,1)S(1)}, u32[]{:S(2)}, u32[]{:S(2)}) collective-permute-start(bf16[512,64]{0,1:T(8,128)(2,1)S(1)} %collective-permute-done.4), channel_id=1, source_target_pairs={{0,128},{16,144},{32,160},{48,176},{64,192},{80,208},{96,224},{112... | collective-permute-start | bytes 196616 | tf_op jit(solution)/shard_map/ppermute | solution.py:15
  73.6 10.1 %collective-permute-start.6 = (bf16[512,64]{0,1:T(8,128)(2,1)S(1)}, bf16[512,64]{0,1:T(8,128)(2,1)S(1)}, u32[]{:S(2)}, u32[]{:S(2)}) collective-permute-start(bf16[512,64]{0,1:T(8,128)(2,1)S(1)} %collective-permute-done.5), channel_id=1, source_target_pairs={{0,256},{16,272},{32,288},{48,304},{64,320},{80,336},{96,352},{112... | collective-permute-start | bytes 196616 | tf_op jit(solution)/shard_map/ppermute | solution.py:15
  84.4 379.1 %reduce-scatter.7.cloned.1.call-start = ((), (), s32[]{:S(2)}) async-start(), calls=%async_computation.7 | async-start | bytes 1114112 | tf_op jit(solution)/shard_map/reduce_scatter | solution.py:123
  161.8 145.9 %collective-permute-start = (bf16[16,8192]{1,0:T(8,128)(2,1)S(1)}, bf16[16,8192]{1,0:T(8,128)(2,1)S(1)}, u32[]{:S(2)}, u32[]{:S(2)}) collective-permute-start(bf16[16,8192]{1,0:T(8,128)(2,1)S(1)} %get-tuple-element.37), channel_id=1, source_target_pairs={{0,16},{16,32},{32,48},{48,64},{64,80},{80,96},{96,112},{112,128},... | collective-permute-start | bytes 786440 | tf_op jit(solution)/shard_map/ppermute | solution.py:21
  318.2 20.2 %collective-permute-start.1 = (bf16[16,8192]{1,0:T(8,128)(2,1)}, bf16[16,8192]{1,0:T(8,128)(2,1)}, u32[]{:S(2)}, u32[]{:S(2)}) collective-permute-start(bf16[16,8192]{1,0:T(8,128)(2,1)} %fusion.5), channel_id=1, source_target_pairs={{0,16},{16,32},{32,48},{48,64},{64,80},{80,96},{96,112},{112,128},... | collective-permute-start | bytes 786440 | tf_op jit(solution)/shard_map/ppermute | solution.py:21
  325.9 12.5 %collective-permute-start.13 = (bf16[16,8192]{1,0:T(8,128)(2,1)}, bf16[16,8192]{1,0:T(8,128)(2,1)S(1)}, u32[]{:S(2)}, u32[]{:S(2)}) collective-permute-start(bf16[16,8192]{1,0:T(8,128)(2,1)} %fusion.8), channel_id=1, source_target_pairs={{16,0},{32,16},{48,32},{64,48},{80,64},{96,80},{112,96},{128,112},... | collective-permute-start | bytes 786440 | tf_op jit(solution)/shard_map/ppermute | solution.py:21
  334.2 7.1 %collective-permute-start.14 = (bf16[16,8192]{1,0:T(8,128)(2,1)S(1)}, bf16[16,8192]{1,0:T(8,128)(2,1)S(1)}, u32[]{:S(2)}, u32[]{:S(2)}) collective-permute-start(bf16[16,8192]{1,0:T(8,128)(2,1)S(1)} %fusion.68), channel_id=1, source_target_pairs={{16,0},{32,16},{48,32},{64,48},{80,64},{96,80},{112,96},{128,112},... | collective-permute-start | bytes 786440 | tf_op jit(solution)/shard_map/ppermute | solution.py:21
  343.1 42.2 %collective-permute-start.15 = (bf16[16,8192]{1,0:T(8,128)(2,1)}, bf16[16,8192]{1,0:T(8,128)(2,1)}, u32[]{:S(2)}, u32[]{:S(2)}) collective-permute-start(bf16[16,8192]{1,0:T(8,128)(2,1)} %fusion.74), channel_id=1, source_target_pairs={{16,0},{32,16},{48,32},{64,48},{80,64},{96,80},{112,96},{128,112},... | collective-permute-start | bytes 786440 | tf_op jit(solution)/shard_map/ppermute | solution.py:21
  350.9 8.0 %collective-permute-start.16 = (bf16[16,8192]{1,0:T(8,128)(2,1)}, bf16[16,8192]{1,0:T(8,128)(2,1)}, u32[]{:S(2)}, u32[]{:S(2)}) collective-permute-start(bf16[16,8192]{1,0:T(8,128)(2,1)} %fusion.86), channel_id=1, source_target_pairs={{0,16},{16,32},{32,48},{48,64},{64,80},{80,96},{96,112},{112,128},... | collective-permute-start | bytes 786440 | tf_op jit(solution)/shard_map/ppermute | solution.py:21
  361.0 7.8 %collective-permute-start.17 = (bf16[16,8192]{1,0:T(8,128)(2,1)S(1)}, bf16[16,8192]{1,0:T(8,128)(2,1)S(1)}, u32[]{:S(2)}, u32[]{:S(2)}) collective-permute-start(bf16[16,8192]{1,0:T(8,128)(2,1)S(1)} %fusion.92), channel_id=1, source_target_pairs={{0,16},{16,32},{32,48},{48,64},{64,80},{80,96},{96,112},{112,128},... | collective-permute-start | bytes 786440 | tf_op jit(solution)/shard_map/ppermute | solution.py:21
  371.4 165.1 %reduce-scatter.11.cloned.1.call-start = ((), (), s32[]{:S(2)}) async-start(), calls=%async_computation.9 | async-start | bytes 1114112 | tf_op jit(solution)/shard_map/reduce_scatter | solution.py:126
  385.2 224.5 %reduce-scatter.5.cloned.1.call-start = ((), (), s32[]{:S(2)}) async-start(), calls=%async_computation.6 | async-start | bytes 1114112 | tf_op jit(solution)/shard_map/reduce_scatter | solution.py:117
  390.5 292.3 %reduce-scatter.9.cloned.1.call-start = ((), (), s32[]{:S(2)}) async-start(), calls=%async_computation.8 | async-start | bytes 1114112 | tf_op jit(solution)/shard_map/reduce_scatter | solution.py:120
  463.4 75.0 %collective-permute-start.18 = (bf16[512,64]{0,1:T(8,128)(2,1)}, bf16[512,64]{0,1:T(8,128)(2,1)S(1)}, u32[]{:S(2)}, u32[]{:S(2)}) collective-permute-start(bf16[512,64]{0,1:T(8,128)(2,1)} %reduce-scatter.7.cloned.1.call-done), channel_id=1, source_target_pairs={{0,16},{16,0},{32,48},{48,32},{64,80},{80,64},{96,112},{112,96},{1... | collective-permute-start | bytes 196616 | tf_op jit(solution)/shard_map/ppermute | solution.py:15
  536.5 6.8 collective-permute-start.23
  538.4 8.5 %collective-permute-start.19 = (bf16[512,64]{0,1:T(8,128)(2,1)S(1)}, bf16[512,64]{0,1:T(8,128)(2,1)}, u32[]{:S(2)}, u32[]{:S(2)}) collective-permute-start(bf16[512,64]{0,1:T(8,128)(2,1)S(1)} %collective-permute-done.18), channel_id=1, source_target_pairs={{0,32},{16,48},{32,0},{48,16},{64,96},{80,112},{96,64},{112,80},{1... | collective-permute-start | bytes 196616 | tf_op jit(solution)/shard_map/ppermute | solution.py:15
  543.3 7.9 %collective-permute-start.24 = (bf16[64,512]{1,0:T(8,128)(2,1)}, bf16[64,512]{1,0:T(8,128)(2,1)S(1)}, u32[]{:S(2)}, u32[]{:S(2)}) collective-permute-start(bf16[64,512]{1,0:T(8,128)(2,1)} %collective-permute-done.23), channel_id=1, source_target_pairs={{0,32},{16,48},{32,0},{48,16},{64,96},{80,112},{96,64},{112,80},{1... | collective-permute-start | bytes 196616 | tf_op jit(solution)/shard_map/ppermute | solution.py:15
  546.9 7.9 %collective-permute-start.20 = (bf16[512,64]{0,1:T(8,128)(2,1)}, bf16[512,64]{0,1:T(8,128)(2,1)S(1)}, u32[]{:S(2)}, u32[]{:S(2)}) collective-permute-start(bf16[512,64]{0,1:T(8,128)(2,1)} %collective-permute-done.19), channel_id=1, source_target_pairs={{0,64},{16,80},{32,96},{48,112},{64,0},{80,16},{96,32},{112,48},{1... | collective-permute-start | bytes 196616 | tf_op jit(solution)/shard_map/ppermute | solution.py:15
  551.3 8.1 %collective-permute-start.25 = (bf16[64,512]{1,0:T(8,128)(2,1)S(1)}, bf16[64,512]{1,0:T(8,128)(2,1)S(1)}, u32[]{:S(2)}, u32[]{:S(2)}) collective-permute-start(bf16[64,512]{1,0:T(8,128)(2,1)S(1)} %collective-permute-done.24), channel_id=1, source_target_pairs={{0,64},{16,80},{32,96},{48,112},{64,0},{80,16},{96,32},{112,48},{1... | collective-permute-start | bytes 196616 | tf_op jit(solution)/shard_map/ppermute | solution.py:15
  554.8 8.7 %collective-permute-start.21 = (bf16[512,64]{0,1:T(8,128)(2,1)S(1)}, bf16[512,64]{0,1:T(8,128)(2,1)S(1)}, u32[]{:S(2)}, u32[]{:S(2)}) collective-permute-start(bf16[512,64]{0,1:T(8,128)(2,1)S(1)} %collective-permute-done.20), channel_id=1, source_target_pairs={{0,128},{16,144},{32,160},{48,176},{64,192},{80,208},{96,224},{112... | collective-permute-start | bytes 196616 | tf_op jit(solution)/shard_map/ppermute | solution.py:15
  559.4 10.4 %collective-permute-start.26 = (bf16[64,512]{1,0:T(8,128)(2,1)S(1)}, bf16[64,512]{1,0:T(8,128)(2,1)S(1)}, u32[]{:S(2)}, u32[]{:S(2)}) collective-permute-start(bf16[64,512]{1,0:T(8,128)(2,1)S(1)} %collective-permute-done.25), channel_id=1, source_target_pairs={{0,128},{16,144},{32,160},{48,176},{64,192},{80,208},{96,224},{112... | collective-permute-start | bytes 196616 | tf_op jit(solution)/shard_map/ppermute | solution.py:15
  563.5 46.3 %collective-permute-start.22 = (bf16[512,64]{0,1:T(8,128)(2,1)S(1)}, bf16[512,64]{0,1:T(8,128)(2,1)S(1)}, u32[]{:S(2)}, u32[]{:S(2)}) collective-permute-start(bf16[512,64]{0,1:T(8,128)(2,1)S(1)} %collective-permute-done.21), channel_id=1, source_target_pairs={{0,256},{16,272},{32,288},{48,304},{64,320},{80,336},{96,352},{112... | collective-permute-start | bytes 196616 | tf_op jit(solution)/shard_map/ppermute | solution.py:15
  569.8 113.1 %collective-permute-start.27 = (bf16[64,512]{1,0:T(8,128)(2,1)S(1)}, bf16[64,512]{1,0:T(8,128)(2,1)S(1)}, u32[]{:S(2)}, u32[]{:S(2)}) collective-permute-start(bf16[64,512]{1,0:T(8,128)(2,1)S(1)} %collective-permute-done.26), channel_id=1, source_target_pairs={{0,256},{16,272},{32,288},{48,304},{64,320},{80,336},{96,352},{112... | collective-permute-start | bytes 196616 | tf_op jit(solution)/shard_map/ppermute | solution.py:15
  (42 other events, 1058.3 us)
Sparse Core Ops, SparseCore 0:
  10.1 77.0 all-gather.12
  89.3 69.0 all-gather.10
  161.0 69.3 all-gather.8
  232.9 69.3 all-gather.6
  371.5 91.8 reduce-scatter.6
  466.3 70.1 reduce-scatter.10
  539.3 70.3 reduce-scatter.4
  612.8 70.0 reduce-scatter.8
where the time goes:
time: 693 us; the launch traced here: 691 us
  waiting for transfers between devices  509 us (73%)
  starting transfers between devices  93.6 us (14%)
  matrix products  50.9 us (7%)
  other arithmetic  19.4 us (3%)
  between operations  14.9 us (2%)
    reduce_scatter x1, waiting for transfers between devices, body(): lax.psum_scatter(sum_in_up.astype(jnp.bfloat16), 'dp', scatter_dimension=...  72.9 us
    ppermute x20, starting transfers between devices, partner(): return lax.ppermute(value, axis, pairs)  72.3 us
    all_gather x1, waiting for transfers between devices, body(): lax.all_gather(twin_in, 'dp', axis=0, tiled=True)  71.9 us
    reduce_scatter x1, waiting for transfers between devices, body(): lax.psum_scatter(sum_out_down.astype(jnp.bfloat16), 'dp', scatter_dimensi...  71.6 us
    all_gather x1, waiting for transfers between devices, body(): lax.all_gather(own_in, 'dp', axis=0, tiled=True)  71.2 us
    reduce_scatter x1, waiting for transfers between devices, body(): lax.psum_scatter(sum_out_up.astype(jnp.bfloat16), 'dp', scatter_dimension...  69.1 us
    all_gather x1, waiting for transfers between devices, body(): lax.all_gather(twin_out, 'dp', axis=1, tiled=True)  66.6 us
    ppermute x20, waiting for transfers between devices, partner(): return lax.ppermute(value, axis, pairs)  37.6 us
  transfers between devices with their start and end apart: 36, of which 23 were waited for; matrix products, arithmetic and copies ran while one was open for 9% of the time, Pallas kernels for 0%

commit v1 on v0

v1 whole, which is shorter than its diff:
```python
import functools

import jax
import jax.numpy as jnp
from jax import lax
from jax.experimental import pallas as pl
from jax.experimental.pallas import tpu as pltpu
from jax.sharding import PartitionSpec as P

TICKS = 3
EPSILON = 1e-05
BF16 = jnp.bfloat16
F32 = jnp.float32

VMEM = pl.BlockSpec(memory_space=pltpu.VMEM)
SMEM = pl.BlockSpec(memory_space=pltpu.SMEM)
PARAMS = pltpu.CompilerParams(vmem_limit_bytes=40 * 2**20)


def nt(a, b):
    return lax.dot_general(a, b, (((1,), (1,)), ((), ())), preferred_element_type=F32)


def nn(a, b):
    return jnp.dot(a, b, preferred_element_type=F32)


def tn(a, b):
    return lax.dot_general(a, b, (((0,), (0,)), ((), ())), preferred_element_type=F32)


def both(parts, cols):
    if len(parts) == 1:
        return parts[0][:, cols]
    return jnp.concatenate([part[:, cols] for part in parts], axis=0)


def project(take, w_ref, half, square):
    blocks, _, wide = w_ref.shape
    rank = w_ref.shape[1] // 2
    total, squares = None, None
    for j in range(blocks):
        x = take(pl.ds(j * wide, wide))
        term = nt(x, w_ref[j, half * rank : (half + 1) * rank, :])
        total = term if total is None else total + term
        if square:
            x = x.astype(F32)
            squares = x * x if squares is None else squares + x * x
    if not square:
        return total
    return total, jnp.sum(squares, axis=-1, keepdims=True)


def forward_kernel(n_parts, flags, *refs):
    parts, rest = refs[:n_parts], refs[n_parts:]
    if n_parts == 1:
        enter_ref, w_ref, y_ref = rest
        first = flags[0] == 1

        def take(cols):
            entering = jnp.concatenate([enter_ref[0, :, cols], enter_ref[1, :, cols]], axis=0)
            return jnp.where(first, entering, parts[0][:, cols])
    else:
        w_ref, y_ref = rest

        def take(cols):
            return both(parts, cols)

    blocks, _, wide = w_ref.shape
    rank = w_ref.shape[1] // 2
    total, squares = project(take, w_ref, 0, True)
    inv_rms = lax.rsqrt(squares / (blocks * wide) + EPSILON)
    pre = total * inv_rms
    hidden = (pre * jax.nn.sigmoid(pre)).astype(BF16)
    for j in range(blocks):
        cols = pl.ds(j * wide, wide)
        y_ref[:, cols] = (take(cols).astype(F32) + nn(hidden, w_ref[j, rank:, :])).astype(BF16)


def backward_kernel(n_x, n_c, moment, flags, sd_ref, su_ref, *refs):
    xs, y_ref, refs = refs[:n_x], refs[n_x], refs[n_x + 1 :]
    cs, (w_ref, g_ref, pre_grad_ref, hidden_ref) = refs[:n_c], refs[n_c:]
    blocks, _, wide = w_ref.shape
    rank = w_ref.shape[1] // 2
    last = flags[1] == 1

    def rows(cols):
        stash = jnp.concatenate([sd_ref[moment, :, cols], su_ref[moment, :, cols]], axis=0)
        return jnp.where(last, both(xs, cols), stash)

    def cot(cols):
        return jnp.where(last, y_ref[:, cols], both(cs, cols))

    total, squares = project(rows, w_ref, 0, True)
    hidden_grad = project(cot, w_ref, 1, False)
    inv_rms = lax.rsqrt(squares / (blocks * wide) + EPSILON)
    pre = total * inv_rms
    sigma = jax.nn.sigmoid(pre)
    hidden_ref[...] = (pre * sigma).astype(BF16)
    pre_grad = (hidden_grad * sigma * (1.0 + pre * (1.0 - sigma))).astype(BF16)
    wide_grad = pre_grad.astype(F32)
    pre_grad_ref[...] = (wide_grad * inv_rms).astype(BF16)
    inner = jnp.sum(wide_grad * pre, axis=-1, keepdims=True) / (blocks * wide)
    back = inv_rms * inv_rms * inner
    for j in range(blocks):
        cols = pl.ds(j * wide, wide)
        normed_grad = nn(pre_grad, w_ref[j, :rank, :])
        g_ref[:, cols] = (
            cot(cols).astype(F32) + inv_rms * normed_grad - back * rows(cols).astype(F32)
        ).astype(BF16)


def terms_kernel(flags, sd_ref, su_ref, *refs):
    xd, xu, cd, cu, x1, x2, c1, c2, y0, y1, y2 = refs[:11]
    pre_grads, hiddens, out_ref = refs[11:14], refs[14:17], refs[17]
    blocks, _, wide = out_ref.shape
    rank = out_ref.shape[1] // 2
    last = flags[1] == 1
    pre_grad = jnp.concatenate([r[...] for r in pre_grads], axis=0)
    hidden = jnp.concatenate([r[...] for r in hiddens], axis=0)
    for j in range(blocks):
        cols = pl.ds(j * wide, wide)
        stash = jnp.concatenate([r[t, :, cols] for t in range(TICKS) for r in (sd_ref, su_ref)], axis=0)
        x = jnp.concatenate([r[:, cols] for r in (xd, xu, x1, x2)], axis=0)
        y = jnp.concatenate([r[:, cols] for r in (y0, y1, y2)], axis=0)
        c = jnp.concatenate([r[:, cols] for r in (cd, cu, c1, c2)], axis=0)
        out_ref[j, :rank, :] = tn(pre_grad, jnp.where(last, x, stash)).astype(BF16)
        out_ref[j, rank:, :] = tn(hidden, jnp.where(last, y, c)).astype(BF16)


def sum_kernel(rank, in_ref, a_ref, b_ref):
    total = in_ref[0].astype(F32)
    for j in range(1, in_ref.shape[0]):
        total = total + in_ref[j].astype(F32)
    a_ref[...] = total[:rank]
    b_ref[...] = total[rank:]


def call(kernel, out, *args, flops=0):
    specs = [SMEM if a.dtype == jnp.int32 else VMEM for a in args]
    outs = out if isinstance(out, (list, tuple)) else [out]
    size = sum(a.size * a.dtype.itemsize for a in list(args) + list(outs))
    return pl.pallas_call(
        kernel,
        out_shape=out,
        in_specs=specs,
        out_specs=jax.tree.map(lambda _: VMEM, out),
        compiler_params=PARAMS,
        cost_estimate=pl.CostEstimate(flops=flops, bytes_accessed=size, transcendentals=0),
    )(*args)


def body(
    adapter_in, adapter_out, down_state, up_state, down_cot, up_cot, down_stash, up_stash, entering
):
    sections = lax.axis_size("section")
    position = lax.axis_index("section")
    flags = jnp.stack([position == 0, position == sections - 1]).astype(jnp.int32)
    mirror = [(s, sections - 1 - s) for s in range(sections)]
    higher = [(s, s + 1) for s in range(sections - 1)]
    lower = [(s + 1, s) for s in range(sections - 1)]
    replicas = lax.axis_size("dp")
    share, rank = adapter_in.shape[1:]
    rows, width = down_state.shape[1:]
    shape = jax.ShapeDtypeStruct

    xd, cd, sd = down_state[0], down_cot[0], down_stash[0]
    xu = lax.ppermute(up_state[0], "section", mirror)
    cu = lax.ppermute(up_cot[0], "section", mirror)
    su = lax.ppermute(up_stash[0], "section", mirror)

    shard = jnp.concatenate([adapter_in[0].T, adapter_out[0]], axis=0)
    weights = lax.all_to_all(
        jnp.broadcast_to(shard[None], (replicas,) + shard.shape), "dp", 0, 0, tiled=True
    )

    one = 2 * 2 * rows * width * rank
    full = shape((2 * rows, width), BF16)
    low = shape((2 * rows, rank), BF16)
    x, c = (xd, xu), (cd, cu)
    xs, ys, cs, pre_grads, hiddens = [], [], [], [], []
    for moment in range(TICKS):
        enter = () if moment == 0 else (entering[:, moment - 1],)
        y = call(
            functools.partial(forward_kernel, len(x)), full, flags, *x, *enter, weights, flops=2 * one
        )
        g, pre_grad, hidden = call(
            functools.partial(backward_kernel, len(x), len(c), moment),
            [full, low, low],
            flags, sd, su, *x, y, *c, weights,
            flops=3 * one,
        )
        xs.append(x)
        ys.append(y)
        cs.append(c)
        pre_grads.append(pre_grad)
        hiddens.append(hidden)
        if moment + 1 < TICKS:
            x = (lax.ppermute(y, "section", higher),)
            c = (lax.ppermute(g, "section", lower),)
    partial = call(
        terms_kernel,
        shape((replicas, 2 * rank, share), BF16),
        flags, sd, su, *xs[0], *cs[0], *xs[1], *xs[2], *cs[1], *cs[2], *ys, *pre_grads, *hiddens,
        flops=6 * one,
    )
    up_out = lax.ppermute(y[rows:], "section", mirror)
    up_back = lax.ppermute(g[rows:], "section", mirror)
    pieces = lax.all_to_all(partial, "dp", 0, 0, tiled=True)
    grad_in, grad_out = call(
        functools.partial(sum_kernel, rank), [shape((rank, share), F32), shape((rank, share), F32)], pieces
    )
    return (y[None, :rows], up_out[None], g[None, :rows], up_back[None], grad_in.T[None], grad_out[None])


def solution(mesh):
    return jax.shard_map(
        body,
        mesh=mesh,
        in_specs=(
            P("section", "dp", None),
            P("section", None, "dp"),
            P("section", "dp", None),
            P("section", "dp", None),
            P("section", "dp", None),
            P("section", "dp", None),
            P("section", None, "dp", None),
            P("section", None, "dp", None),
            P(None, None, "dp", None),
        ),
        out_specs=(
            P("section", "dp", None),
            P("section", "dp", None),
            P("section", "dp", None),
            P("section", "dp", None),
            P("section", "dp", None),
            P("section", None, "dp"),
        ),
        check_vma=False,
    )
```

time: 693 us -> 179 us (0.26)
  the two profiles are of different devices: /device:TPU:2 before, /device:TPU:135 now
where the time goes in v1:
time: 179 us; the launch traced here: 178 us
  waiting for transfers between devices  86.5 us (48%)
  starting transfers between devices  68.9 us (38%)
  Pallas kernels  14.2 us (8%)
  local copies, waits for them, and re-layouts  6.67 us (4%)
    ppermute x1, waiting for transfers between devices, body(): xu = lax.ppermute(up_state[0], 'section', mirror)  44.6 us
    ppermute x2, waiting for transfers between devices, body(): c = (lax.ppermute(g, 'section', lower),)  22.2 us
    all_to_all x1, starting transfers between devices, body(): pieces = lax.all_to_all(partial, 'dp', 0, 0, tiled=True)  18.6 us
    pallas_call x8, Pallas kernels, call(): pl.pallas_call(kernel, out_shape=out, in_specs=specs, out_specs=jax.tree....  14.2 us
    ppermute x2, starting transfers between devices, body(): x = (lax.ppermute(y, 'section', higher),)  10.4 us
    all_to_all x1, starting transfers between devices, body(): lax.all_to_all(jnp.broadcast_to(shard[None], (replicas,) + shard.shape),...  8.87 us
    ppermute x1, waiting for transfers between devices, body(): up_back = lax.ppermute(g[rows:], 'section', mirror)  7.95 us
    ppermute x1, starting transfers between devices, body(): up_out = lax.ppermute(y[rows:], 'section', mirror)  7.85 us
  transfers between devices with their start and end apart: 11, of which 7 were waited for; matrix products, arithmetic and copies ran while one was open for 1% of the time, Pallas kernels for 5%

profile of v1, /device:TPU:135, one launch (start us, length us, event | category | flops | bytes accessed | tf_op | source)
XLA Modules:
  0.0 178.0 jit_solution(15836157590344993951)
XLA Ops:
  0.6 0.9 pad_maximum_fusion
  1.5 1.5 broadcast_in_dim.24
  3.1 8.9 %all-to-all-start = ((bf16[16,128,512]{2,1,0:T(8,128)(2,1)}), bf16[16,128,512]{2,1,0:T(8,128)(2,1)S(1)}, u32[]{:S(2)}, u32[]{:S(2)}) async-start(bf16[16,128,512]{2,1,0:T(8,128)(2,1)} %broadcast_in_dim.24), calls=%async_computation | async-start | bytes 4194304 | tf_op jit(solution)/shard_map/all_to_all | solution.py:173
  11.9 7.0 %collective-permute-start.4 = (bf16[3,16,8192]{2,1,0:T(8,128)(2,1)}, bf16[3,16,8192]{2,1,0:T(8,128)(2,1)}, u32[]{:S(2)}, u32[]{:S(2)}) collective-permute-start(bf16[3,16,8192]{2,1,0:T(8,128)(2,1)} %bitcast.43), channel_id=1, source_target_pairs={{0,496},{16,480},{32,464},{48,448},{64,432},{80,416},{96,400},{112... | collective-permute-start | bytes 2359304 | tf_op jit(solution)/shard_map/ppermute | solution.py:170
  19.0 2.9 %collective-permute-start = (bf16[16,8192]{1,0:T(8,128)(2,1)}, bf16[16,8192]{1,0:T(8,128)(2,1)S(1)}, u32[]{:S(2)}, u32[]{:S(2)}) collective-permute-start(bf16[16,8192]{1,0:T(8,128)(2,1)} %bitcast.44), channel_id=1, source_target_pairs={{0,496},{16,480},{32,464},{48,448},{64,432},{80,416},{96,400},{112... | collective-permute-start | bytes 786440 | tf_op jit(solution)/shard_map/ppermute | solution.py:168
  21.9 6.9 %collective-permute-start.5 = (bf16[16,8192]{1,0:T(8,128)(2,1)}, bf16[16,8192]{1,0:T(8,128)(2,1)}, u32[]{:S(2)}, u32[]{:S(2)}) collective-permute-start(bf16[16,8192]{1,0:T(8,128)(2,1)} %bitcast.45), channel_id=1, source_target_pairs={{0,496},{16,480},{32,464},{48,448},{64,432},{80,416},{96,400},{112... | collective-permute-start | bytes 786440 | tf_op jit(solution)/shard_map/ppermute | solution.py:169
  28.9 44.6 %collective-permute-done.refs_1_ = bf16[16,8192]{1,0:T(8,128)(2,1)S(1)} collective-permute-done((bf16[16,8192]{1,0:T(8,128)(2,1)}, bf16[16,8192]{1,0:T(8,128)(2,1)S(1)}, u32[]{:S(2)}, u32[]{:S(2)}) %collective-permute-start) | collective-permute-done | bytes 262176 | tf_op jit(solution)/shard_map/ppermute | solution.py:168
  73.5 1.5 shard_map.136.refs_2_.refs_8_
  74.9 1.9 %collective-permute-start.1 = (bf16[32,8192]{1,0:T(8,128)(2,1)S(1)}, bf16[32,8192]{1,0:T(8,128)(2,1)S(1)}, u32[]{:S(2)}, u32[]{:S(2)}) collective-permute-start(bf16[32,8192]{1,0:T(8,128)(2,1)S(1)} %shard_map.136.refs_2_.refs_8_), channel_id=1, source_target_pairs={{0,16},{16,32},{32,48},{48,64},{64,80},{80,96},{96,112},{112,128},... | collective-permute-start | bytes 1572872 | tf_op jit(solution)/shard_map/ppermute | solution.py:199
  76.9 2.3 %collective-permute-done.5.refs_4_.refs_3_ = bf16[16,8192]{1,0:T(8,128)(2,1)} collective-permute-done((bf16[16,8192]{1,0:T(8,128)(2,1)}, bf16[16,8192]{1,0:T(8,128)(2,1)}, u32[]{:S(2)}, u32[]{:S(2)}) %collective-permute-start.5) | collective-permute-done | bytes 262176 | tf_op jit(solution)/shard_map/ppermute | solution.py:169
  79.2 2.4 %shard_map.139 = (bf16[32,8192]{1,0:T(8,128)(2,1)S(1)}, bf16[32,64]{1,0:T(8,128)(2,1)S(1)}, bf16[32,64]{1,0:T(8,128)(2,1)S(1)}) custom-call(s32[2]{0:T(128)S(1)} %add_convert_fusion.flags, bf16[3,16,8192]{2,1,0:T(8,128)(2,1)S(1)} %bitcast.30, bf16[3,16,8192]{2,1,0:T(8,128)(2,1)} %collective-permute-done.4.su_ref, bf16[16,8192]{1,0:T(8,128)(2,1)S(1)} %bitcast.35, ...), custom_call_target="tpu_custom_call" | custom-call | flops 100663296 | bytes 5775368 | tf_op jit(solution)/shard_map/pallas_call | solution.py:143
  81.6 2.6 %collective-permute-start.6 = (bf16[32,8192]{1,0:T(8,128)(2,1)S(1)}, bf16[32,8192]{1,0:T(8,128)(2,1)S(1)}, u32[]{:S(2)}, u32[]{:S(2)}) collective-permute-start(bf16[32,8192]{1,0:T(8,128)(2,1)S(1)} %get-tuple-element.17), channel_id=1, source_target_pairs={{16,0},{32,16},{48,32},{64,48},{80,64},{96,80},{112,96},{128,112},... | collective-permute-start | bytes 1572872 | tf_op jit(solution)/shard_map/ppermute | solution.py:200
  84.3 1.5 shard_map.137.refs_1_.refs_9_
  85.8 8.5 %collective-permute-start.2 = (bf16[32,8192]{1,0:T(8,128)(2,1)S(1)}, bf16[32,8192]{1,0:T(8,128)(2,1)S(1)}, u32[]{:S(2)}, u32[]{:S(2)}) collective-permute-start(bf16[32,8192]{1,0:T(8,128)(2,1)S(1)} %shard_map.137.refs_1_.refs_9_), channel_id=1, source_target_pairs={{0,16},{16,32},{32,48},{48,64},{64,80},{80,96},{96,112},{112,128},... | collective-permute-start | bytes 1572872 | tf_op jit(solution)/shard_map/ppermute | solution.py:199
  94.3 7.7 %collective-permute-done.6.refs_2_.refs_6_ = bf16[32,8192]{1,0:T(8,128)(2,1)S(1)} collective-permute-done((bf16[32,8192]{1,0:T(8,128)(2,1)S(1)}, bf16[32,8192]{1,0:T(8,128)(2,1)S(1)}, u32[]{:S(2)}, u32[]{:S(2)}) %collective-permute-start.6) | collective-permute-done | bytes 524320 | tf_op jit(solution)/shard_map/ppermute | solution.py:200
  102.0 2.2 %shard_map.140 = (bf16[32,8192]{1,0:T(8,128)(2,1)S(1)}, bf16[32,64]{1,0:T(8,128)(2,1)S(1)}, bf16[32,64]{1,0:T(8,128)(2,1)S(1)}) custom-call(s32[2]{0:T(128)S(1)} %add_convert_fusion.flags, bf16[3,16,8192]{2,1,0:T(8,128)(2,1)S(1)} %bitcast.31, bf16[3,16,8192]{2,1,0:T(8,128)(2,1)} %collective-permute-done.4.su_ref, ...), custom_call_target="tpu_custom_call" | custom-call | flops 100663296 | bytes 5775368 | tf_op jit(solution)/shard_map/pallas_call | solution.py:143
  104.2 1.9 %collective-permute-start.7 = (bf16[32,8192]{1,0:T(8,128)(2,1)S(1)}, bf16[32,8192]{1,0:T(8,128)(2,1)S(1)}, u32[]{:S(2)}, u32[]{:S(2)}) collective-permute-start(bf16[32,8192]{1,0:T(8,128)(2,1)S(1)} %get-tuple-element.18), channel_id=1, source_target_pairs={{16,0},{32,16},{48,32},{64,48},{80,64},{96,80},{112,96},{128,112},... | collective-permute-start | bytes 1572872 | tf_op jit(solution)/shard_map/ppermute | solution.py:200
  106.2 1.5 shard_map.138.refs_1_.refs_10_
  107.7 14.4 %collective-permute-done.7.refs_2_.refs_7_ = bf16[32,8192]{1,0:T(8,128)(2,1)S(1)} collective-permute-done((bf16[32,8192]{1,0:T(8,128)(2,1)S(1)}, bf16[32,8192]{1,0:T(8,128)(2,1)S(1)}, u32[]{:S(2)}, u32[]{:S(2)}) %collective-permute-start.7) | collective-permute-done | bytes 524320 | tf_op jit(solution)/shard_map/ppermute | solution.py:200
  122.1 2.2 %shard_map.141 = (bf16[32,8192]{1,0:T(8,128)(2,1)S(1)}, bf16[32,64]{1,0:T(8,128)(2,1)S(1)}, bf16[32,64]{1,0:T(8,128)(2,1)S(1)}) custom-call(s32[2]{0:T(128)S(1)} %add_convert_fusion.flags, bf16[3,16,8192]{2,1,0:T(8,128)(2,1)S(1)} %bitcast.32, bf16[3,16,8192]{2,1,0:T(8,128)(2,1)} %collective-permute-done.4.su_ref, ...), custom_call_target="tpu_custom_call" | custom-call | flops 100663296 | bytes 5775368 | tf_op jit(solution)/shard_map/pallas_call | solution.py:143
  124.3 0.8 copy-done.7
  125.2 2.0 %shard_map.142 = bf16[16,128,512]{2,1,0:T(8,128)(2,1)S(1)} custom-call(s32[2]{0:T(128)S(1)} %add_convert_fusion.flags, bf16[3,16,8192]{2,1,0:T(8,128)(2,1)S(1)} %bitcast.33, bf16[3,16,8192]{2,1,0:T(8,128)(2,1)} %collective-permute-done.4.su_ref, bf16[16,8192]{1,0:T(8,128)(2,1)S(1)} %bitcast.36, bf16[16,8192]{1,0:T(8,128)(2,1)S(1)} %copy-done.5, ...), custom_call_target="tpu_custom_call" | custom-call | flops 201326592 | bytes 8413192 | tf_op jit(solution)/shard_map/pallas_call | solution.py:143
  127.1 1.3 copy-done.1
  128.5 18.6 %all-to-all-start.1 = ((bf16[16,128,512]{2,1,0:T(8,128)(2,1)}), bf16[16,128,512]{2,1,0:T(8,128)(2,1)S(1)}, u32[]{:S(2)}, u32[]{:S(2)}) async-start(bf16[16,128,512]{2,1,0:T(8,128)(2,1)} %copy-done.1), calls=%async_computation.1 | async-start | bytes 4194304 | tf_op jit(solution)/shard_map/all_to_all | solution.py:209
  147.1 0.7 fusion
  147.8 1.9 %collective-permute-start.8 = (bf16[16,8192]{1,0:T(8,128)(2,1)S(1)}, bf16[16,8192]{1,0:T(8,128)(2,1)S(1)}, u32[]{:S(2)}, u32[]{:S(2)}) collective-permute-start(bf16[16,8192]{1,0:T(8,128)(2,1)S(1)} %get-tuple-element.30), channel_id=1, source_target_pairs={{0,496},{16,480},{32,464},{48,448},{64,432},{80,416},{96,400},{112... | collective-permute-start | bytes 786440 | tf_op jit(solution)/shard_map/ppermute | solution.py:208
  149.7 0.7 fusion.1
  150.5 7.8 %collective-permute-start.3 = (bf16[16,8192]{1,0:T(8,128)(2,1)S(1)}, bf16[16,8192]{1,0:T(8,128)(2,1)S(1)}, u32[]{:S(2)}, u32[]{:S(2)}) collective-permute-start(bf16[16,8192]{1,0:T(8,128)(2,1)S(1)} %get-tuple-element.32), channel_id=1, source_target_pairs={{0,496},{16,480},{32,464},{48,448},{64,432},{80,416},{96,400},{112... | collective-permute-start | bytes 786440 | tf_op jit(solution)/shard_map/ppermute | solution.py:207
  158.3 8.0 %collective-permute-done.8 = bf16[16,8192]{1,0:T(8,128)(2,1)S(1)} collective-permute-done((bf16[16,8192]{1,0:T(8,128)(2,1)S(1)}, bf16[16,8192]{1,0:T(8,128)(2,1)S(1)}, u32[]{:S(2)}, u32[]{:S(2)}) %collective-permute-start.8) | collective-permute-done | bytes 262176 | tf_op jit(solution)/shard_map/ppermute | solution.py:208
  166.3 3.2 %collective-permute-done.3 = bf16[16,8192]{1,0:T(8,128)(2,1)S(1)} collective-permute-done((bf16[16,8192]{1,0:T(8,128)(2,1)S(1)}, bf16[16,8192]{1,0:T(8,128)(2,1)S(1)}, u32[]{:S(2)}, u32[]{:S(2)}) %collective-permute-start.3) | collective-permute-done | bytes 262176 | tf_op jit(solution)/shard_map/ppermute | solution.py:207
  169.4 6.3 %all-to-all-done.1.in_ref = bf16[16,128,512]{2,1,0:T(8,128)(2,1)S(1)} async-done(((bf16[16,128,512]{2,1,0:T(8,128)(2,1)}), bf16[16,128,512]{2,1,0:T(8,128)(2,1)S(1)}, u32[]{:S(2)}, u32[]{:S(2)}) %all-to-all-start.1) | async-done | bytes 2097184 | tf_op jit(solution)/shard_map/all_to_all | solution.py:209
  175.7 0.9 shard_map.143
  (26 shorter events, 1.6 us)
Async XLA Ops:
  3.1 70.4 %copy-start.2 = (bf16[1,16,8192]{2,1,0:T(8,128)(2,1)S(1)}, bf16[1,16,8192]{2,1,0:T(8,128)(2,1)}, u32[]{:S(2)}) copy-start(bf16[1,16,8192]{2,1,0:T(8,128)(2,1)} %param.11) | copy-start | bytes 786436
  3.1 70.4 %all-to-all-start = ((bf16[16,128,512]{2,1,0:T(8,128)(2,1)}), bf16[16,128,512]{2,1,0:T(8,128)(2,1)S(1)}, u32[]{:S(2)}, u32[]{:S(2)}) async-start(bf16[16,128,512]{2,1,0:T(8,128)(2,1)} %broadcast_in_dim.24), calls=%async_computation | async-start | bytes 4194304 | tf_op jit(solution)/shard_map/all_to_all | solution.py:173
  11.9 67.2 %copy-start = (bf16[1,3,16,8192]{3,2,1,0:T(8,128)(2,1)S(1)}, bf16[1,3,16,8192]{3,2,1,0:T(8,128)(2,1)}, u32[]{:S(2)}) copy-start(bf16[1,3,16,8192]{3,2,1,0:T(8,128)(2,1)} %param.15) | copy-start | bytes 2359300
  11.9 67.2 %collective-permute-start.4 = (bf16[3,16,8192]{2,1,0:T(8,128)(2,1)}, bf16[3,16,8192]{2,1,0:T(8,128)(2,1)}, u32[]{:S(2)}, u32[]{:S(2)}) collective-permute-start(bf16[3,16,8192]{2,1,0:T(8,128)(2,1)} %bitcast.43), channel_id=1, source_target_pairs={{0,496},{16,480},{32,464},{48,448},{64,432},{80,416},{96,400},{112... | collective-permute-start | bytes 2359304 | tf_op jit(solution)/shard_map/ppermute | solution.py:170
  19.0 54.5 %collective-permute-start = (bf16[16,8192]{1,0:T(8,128)(2,1)}, bf16[16,8192]{1,0:T(8,128)(2,1)S(1)}, u32[]{:S(2)}, u32[]{:S(2)}) collective-permute-start(bf16[16,8192]{1,0:T(8,128)(2,1)} %bitcast.44), channel_id=1, source_target_pairs={{0,496},{16,480},{32,464},{48,448},{64,432},{80,416},{96,400},{112... | collective-permute-start | bytes 786440 | tf_op jit(solution)/shard_map/ppermute | solution.py:168
  21.9 57.3 %collective-permute-start.5 = (bf16[16,8192]{1,0:T(8,128)(2,1)}, bf16[16,8192]{1,0:T(8,128)(2,1)}, u32[]{:S(2)}, u32[]{:S(2)}) collective-permute-start(bf16[16,8192]{1,0:T(8,128)(2,1)} %bitcast.45), channel_id=1, source_target_pairs={{0,496},{16,480},{32,464},{48,448},{64,432},{80,416},{96,400},{112... | collective-permute-start | bytes 786440 | tf_op jit(solution)/shard_map/ppermute | solution.py:169
  73.4 8.2 %copy-start.4 = (bf16[16,8192]{1,0:T(8,128)(2,1)}, bf16[16,8192]{1,0:T(8,128)(2,1)S(1)}, u32[]{:S(2)}) copy-start(bf16[16,8192]{1,0:T(8,128)(2,1)S(1)} %collective-permute-done.refs_1_) | copy-start | bytes 786436
  73.4 5.7 %copy-start.6 = (bf16[1,16,8192]{2,1,0:T(8,128)(2,1)S(1)}, bf16[1,16,8192]{2,1,0:T(8,128)(2,1)}, u32[]{:S(2)}) copy-start(bf16[1,16,8192]{2,1,0:T(8,128)(2,1)} %param.13) | copy-start | bytes 786436
  74.9 9.4 %collective-permute-start.1 = (bf16[32,8192]{1,0:T(8,128)(2,1)S(1)}, bf16[32,8192]{1,0:T(8,128)(2,1)S(1)}, u32[]{:S(2)}, u32[]{:S(2)}) collective-permute-start(bf16[32,8192]{1,0:T(8,128)(2,1)S(1)} %shard_map.136.refs_2_.refs_8_), channel_id=1, source_target_pairs={{0,16},{16,32},{32,48},{48,64},{64,80},{80,96},{96,112},{112,128},... | collective-permute-start | bytes 1572872 | tf_op jit(solution)/shard_map/ppermute | solution.py:199
  79.2 5.0 %copy-start.9 = (bf16[2,2,16,8192]{3,2,1,0:T(8,128)(2,1)S(1)}, bf16[2,2,16,8192]{3,2,1,0:T(8,128)(2,1)}, u32[]{:S(2)}) copy-start(bf16[2,2,16,8192]{3,2,1,0:T(8,128)(2,1)} %param.17) | copy-start | bytes 3145732
  81.6 20.4 %collective-permute-start.6 = (bf16[32,8192]{1,0:T(8,128)(2,1)S(1)}, bf16[32,8192]{1,0:T(8,128)(2,1)S(1)}, u32[]{:S(2)}, u32[]{:S(2)}) collective-permute-start(bf16[32,8192]{1,0:T(8,128)(2,1)S(1)} %get-tuple-element.17), channel_id=1, source_target_pairs={{16,0},{32,16},{48,32},{64,48},{80,64},{96,80},{112,96},{128,112},... | collective-permute-start | bytes 1572872 | tf_op jit(solution)/shard_map/ppermute | solution.py:200
  85.8 20.4 %collective-permute-start.2 = (bf16[32,8192]{1,0:T(8,128)(2,1)S(1)}, bf16[32,8192]{1,0:T(8,128)(2,1)S(1)}, u32[]{:S(2)}, u32[]{:S(2)}) collective-permute-start(bf16[32,8192]{1,0:T(8,128)(2,1)S(1)} %shard_map.137.refs_1_.refs_9_), channel_id=1, source_target_pairs={{0,16},{16,32},{32,48},{48,64},{64,80},{80,96},{96,112},{112,128},... | collective-permute-start | bytes 1572872 | tf_op jit(solution)/shard_map/ppermute | solution.py:199
  104.2 17.8 %collective-permute-start.7 = (bf16[32,8192]{1,0:T(8,128)(2,1)S(1)}, bf16[32,8192]{1,0:T(8,128)(2,1)S(1)}, u32[]{:S(2)}, u32[]{:S(2)}) collective-permute-start(bf16[32,8192]{1,0:T(8,128)(2,1)S(1)} %get-tuple-element.18), channel_id=1, source_target_pairs={{16,0},{32,16},{48,32},{64,48},{80,64},{96,80},{112,96},{128,112},... | collective-permute-start | bytes 1572872 | tf_op jit(solution)/shard_map/ppermute | solution.py:200
  107.6 17.5 %copy-start.3 = (bf16[1,16,8192]{2,1,0:T(8,128)(2,1)S(1)}, bf16[1,16,8192]{2,1,0:T(8,128)(2,1)}, u32[]{:S(2)}) copy-start(bf16[1,16,8192]{2,1,0:T(8,128)(2,1)} %param.11) | copy-start | bytes 786436
  107.6 17.5 %copy-start.5 = (bf16[16,8192]{1,0:T(8,128)(2,1)S(1)}, bf16[16,8192]{1,0:T(8,128)(2,1)}, u32[]{:S(2)}) copy-start(bf16[16,8192]{1,0:T(8,128)(2,1)} %copy-done.4) | copy-start | bytes 786436
  124.3 0.8 copy-start.7
  127.1 1.3 copy-start.1
  128.5 18.6 %copy-start.8 = (bf16[32,8192]{1,0:T(8,128)(2,1)S(1)}, bf16[32,8192]{1,0:T(8,128)(2,1)}, u32[]{:S(2)}) copy-start(bf16[32,8192]{1,0:T(8,128)(2,1)} %copy-done.7) | copy-start | bytes 1572868
  128.5 47.2 %all-to-all-start.1 = ((bf16[16,128,512]{2,1,0:T(8,128)(2,1)}), bf16[16,128,512]{2,1,0:T(8,128)(2,1)S(1)}, u32[]{:S(2)}, u32[]{:S(2)}) async-start(bf16[16,128,512]{2,1,0:T(8,128)(2,1)} %copy-done.1), calls=%async_computation.1 | async-start | bytes 4194304 | tf_op jit(solution)/shard_map/all_to_all | solution.py:209
  147.8 18.5 %collective-permute-start.8 = (bf16[16,8192]{1,0:T(8,128)(2,1)S(1)}, bf16[16,8192]{1,0:T(8,128)(2,1)S(1)}, u32[]{:S(2)}, u32[]{:S(2)}) collective-permute-start(bf16[16,8192]{1,0:T(8,128)(2,1)S(1)} %get-tuple-element.30), channel_id=1, source_target_pairs={{0,496},{16,480},{32,464},{48,448},{64,432},{80,416},{96,400},{112... | collective-permute-start | bytes 786440 | tf_op jit(solution)/shard_map/ppermute | solution.py:208
  150.5 19.0 %collective-permute-start.3 = (bf16[16,8192]{1,0:T(8,128)(2,1)S(1)}, bf16[16,8192]{1,0:T(8,128)(2,1)S(1)}, u32[]{:S(2)}, u32[]{:S(2)}) collective-permute-start(bf16[16,8192]{1,0:T(8,128)(2,1)S(1)} %get-tuple-element.32), channel_id=1, source_target_pairs={{0,496},{16,480},{32,464},{48,448},{64,432},{80,416},{96,400},{112... | collective-permute-start | bytes 786440 | tf_op jit(solution)/shard_map/ppermute | solution.py:207

commit v2 on v1

v2 whole, which is shorter than its diff:
```python
import functools

import jax
import jax.numpy as jnp
from jax import lax
from jax.experimental import pallas as pl
from jax.experimental.pallas import tpu as pltpu
from jax.sharding import PartitionSpec as P

TICKS = 3
EPSILON = 1e-05
BF16 = jnp.bfloat16
F32 = jnp.float32

VMEM = pl.BlockSpec(memory_space=pltpu.VMEM)
SMEM = pl.BlockSpec(memory_space=pltpu.SMEM)
PLAIN = pl.BlockSpec()
PARAMS = pltpu.CompilerParams(vmem_limit_bytes=40 * 2**20)


def nt(a, b):
    return lax.dot_general(a, b, (((1,), (1,)), ((), ())), preferred_element_type=F32)


def nn(a, b):
    return jnp.dot(a, b, preferred_element_type=F32)


def tn(a, b):
    return lax.dot_general(a, b, (((0,), (0,)), ((), ())), preferred_element_type=F32)


def both(parts, spot, cols):
    if len(parts) == 1:
        return parts[0][:, cols]
    return jnp.concatenate([parts[0][:, cols], parts[1][spot, :, cols]], axis=0)


def stacked(refs, cols):
    return jnp.concatenate([ref[:, cols] for ref in refs], axis=0)


def put(refs, cols, value):
    count = value.shape[0] // len(refs)
    for i, ref in enumerate(refs):
        ref[:, cols] = value[i * count : (i + 1) * count]


def project(take, w_ref, half, square):
    blocks, _, wide = w_ref.shape
    rank = w_ref.shape[1] // 2
    total, squares = None, None
    for j in range(blocks):
        x = take(pl.ds(j * wide, wide))
        term = nt(x, w_ref[j, half * rank : (half + 1) * rank, :])
        total = term if total is None else total + term
        if square:
            x = x.astype(F32)
            squares = x * x if squares is None else squares + x * x
    if not square:
        return total
    return total, jnp.sum(squares, axis=-1, keepdims=True)


def forward_kernel(n_parts, flags, *refs):
    parts, rest = refs[:n_parts], refs[n_parts:]
    if n_parts == 1:
        enter_ref, w_ref, *y_refs = rest
        first = flags[0] == 1

        def take(cols):
            entering = jnp.concatenate([enter_ref[0, :, cols], enter_ref[1, :, cols]], axis=0)
            return jnp.where(first, entering, parts[0][:, cols])
    else:
        w_ref, *y_refs = rest

        def take(cols):
            return both(parts, 0, cols)

    blocks, _, wide = w_ref.shape
    rank = w_ref.shape[1] // 2
    total, squares = project(take, w_ref, 0, True)
    inv_rms = lax.rsqrt(squares / (blocks * wide) + EPSILON)
    pre = total * inv_rms
    hidden = (pre * jax.nn.sigmoid(pre)).astype(BF16)
    for j in range(blocks):
        cols = pl.ds(j * wide, wide)
        put(y_refs, cols, (take(cols).astype(F32) + nn(hidden, w_ref[j, rank:, :])).astype(BF16))


def backward_kernel(n_x, n_y, n_c, moment, spot, flags, sd_ref, su_ref, *refs):
    xs, ys, refs = refs[:n_x], refs[n_x : n_x + n_y], refs[n_x + n_y :]
    cs, (w_ref, pre_grad_ref, hidden_ref, *g_refs) = refs[:n_c], refs[n_c:]
    blocks, _, wide = w_ref.shape
    rank = w_ref.shape[1] // 2
    last = flags[1] == 1

    def rows(cols):
        stash = jnp.concatenate([sd_ref[moment, :, cols], su_ref[spot, :, cols]], axis=0)
        return jnp.where(last, both(xs, 0, cols), stash)

    def cot(cols):
        return jnp.where(last, stacked(ys, cols), both(cs, 0, cols))

    total, squares = project(rows, w_ref, 0, True)
    hidden_grad = project(cot, w_ref, 1, False)
    inv_rms = lax.rsqrt(squares / (blocks * wide) + EPSILON)
    pre = total * inv_rms
    sigma = jax.nn.sigmoid(pre)
    hidden_ref[...] = (pre * sigma).astype(BF16)
    pre_grad = (hidden_grad * sigma * (1.0 + pre * (1.0 - sigma))).astype(BF16)
    wide_grad = pre_grad.astype(F32)
    pre_grad_ref[...] = (wide_grad * inv_rms).astype(BF16)
    inner = jnp.sum(wide_grad * pre, axis=-1, keepdims=True) / (blocks * wide)
    back = inv_rms * inv_rms * inner
    for j in range(blocks):
        cols = pl.ds(j * wide, wide)
        normed_grad = nn(pre_grad, w_ref[j, :rank, :])
        g = cot(cols).astype(F32) + inv_rms * normed_grad - back * rows(cols).astype(F32)
        put(g_refs, cols, g.astype(BF16))


def terms_kernel(flags, sd_ref, first_ref, later_ref, *refs):
    xd, xu, cd, cu, x1, x2, c1, c2, y0, y1, y2_down, y2_up = refs[:12]
    pre_grads, hiddens, out_ref = refs[12:15], refs[15:18], refs[18]
    blocks, rank, wide = out_ref.shape
    rank = rank // 2
    last = flags[1] == 1
    pre_grad = jnp.concatenate([r[...] for r in pre_grads], axis=0)
    hidden = jnp.concatenate([r[...] for r in hiddens], axis=0)
    for j in range(blocks):
        cols = pl.ds(j * wide, wide)
        stash = jnp.concatenate(
            [sd_ref[0, :, cols], first_ref[0, :, cols], sd_ref[1, :, cols], later_ref[0, :, cols]]
            + [sd_ref[2, :, cols], later_ref[1, :, cols]],
            axis=0,
        )
        x = jnp.concatenate([xd[:, cols], xu[0, :, cols], x1[:, cols], x2[:, cols]], axis=0)
        y = stacked((y0, y1, y2_down, y2_up), cols)
        c = jnp.concatenate([cd[:, cols], cu[0, :, cols], c1[:, cols], c2[:, cols]], axis=0)
        out_ref[j, :rank, :] = tn(pre_grad, jnp.where(last, x, stash)).astype(BF16)
        out_ref[j, rank:, :] = tn(hidden, jnp.where(last, y, c)).astype(BF16)


def sum_kernel(rank, in_ref, y_ref, g_ref, a_ref, b_ref, y_out, g_out):
    total = in_ref[0].astype(F32)
    for j in range(1, in_ref.shape[0]):
        total = total + in_ref[j].astype(F32)
    a_ref[...] = total[:rank]
    b_ref[...] = total[rank:]
    y_out[...] = y_ref[...]
    g_out[...] = g_ref[...]


def call(kernel, out, *args, flops=0, out_specs=None):
    specs = [SMEM if a.dtype == jnp.int32 else VMEM for a in args]
    outs = out if isinstance(out, (list, tuple)) else [out]
    size = sum(a.size * a.dtype.itemsize for a in list(args) + list(outs))
    return pl.pallas_call(
        kernel,
        out_shape=out,
        in_specs=specs,
        out_specs=jax.tree.map(lambda _: VMEM, out) if out_specs is None else out_specs,
        compiler_params=PARAMS,
        cost_estimate=pl.CostEstimate(flops=flops, bytes_accessed=size, transcendentals=0),
    )(*args)


def body(
    adapter_in, adapter_out, down_state, up_state, down_cot, up_cot, down_stash, up_stash, entering
):
    sections = lax.axis_size("section")
    position = lax.axis_index("section")
    flags = jnp.stack([position == 0, position == sections - 1]).astype(jnp.int32)
    mirror = [(s, sections - 1 - s) for s in range(sections)]
    higher = [(s, s + 1) for s in range(sections - 1)]
    lower = [(s + 1, s) for s in range(sections - 1)]
    replicas = lax.axis_size("dp")
    share, rank = adapter_in.shape[1:]
    rows, width = down_state.shape[1:]
    shape = jax.ShapeDtypeStruct

    xd, cd, sd = down_state[0], down_cot[0], down_stash[0]
    first = lax.ppermute(up_stash[0, 0], "section", mirror)
    xu = lax.ppermute(up_state[0], "section", mirror)
    cu = lax.ppermute(up_cot[0], "section", mirror)
    later = lax.ppermute(up_stash[0, 1:], "section", mirror)
    su = [first[None], later, later]
    spots = [0, 0, 1]

    shard = jnp.concatenate([adapter_in[0].T, adapter_out[0]], axis=0)
    weights = lax.all_to_all(
        jnp.broadcast_to(shard[None], (replicas,) + shard.shape), "dp", 0, 0, tiled=True
    )

    x0, c0 = xu[None], cu[None]
    one = 2 * 2 * rows * width * rank
    full = shape((2 * rows, width), BF16)
    half = shape((rows, width), BF16)
    low = shape((2 * rows, rank), BF16)
    x, c = (xd, xu[None]), (cd, cu[None])
    xs, ys, cs, pre_grads, hiddens = [], [], [], [], []
    for moment in range(TICKS):
        enter = () if moment == 0 else (entering[:, moment - 1],)
        ends = moment + 1 == TICKS
        outs, plain = ([half, half], [PLAIN, PLAIN]) if ends else ([full], [VMEM])
        y = call(
            functools.partial(forward_kernel, len(x)),
            outs, flags, *x, *enter, weights,
            flops=2 * one, out_specs=plain,
        )
        pre_grad, hidden, *g = call(
            functools.partial(backward_kernel, len(x), len(y), len(c), moment, spots[moment]),
            [low, low] + outs,
            flags, sd, su[moment], *x, *y, *c, weights,
            flops=3 * one, out_specs=[VMEM, VMEM] + plain,
        )
        xs.append(x)
        ys.append(y)
        cs.append(c)
        pre_grads.append(pre_grad)
        hiddens.append(hidden)
        if moment + 1 < TICKS:
            x = (lax.ppermute(y[0], "section", higher),)
            c = (lax.ppermute(g[0], "section", lower),)
    partial = call(
        terms_kernel,
        shape((replicas, 2 * rank, share), BF16),
        flags, sd, su[0], later, xd, x0, cd, c0, *xs[1], *xs[2], *cs[1], *cs[2], *ys[0], *ys[1], *ys[2], *pre_grads, *hiddens,
        flops=6 * one,
    )
    up_out = lax.ppermute(y[1], "section", mirror)
    up_back = lax.ppermute(g[1], "section", mirror)
    pieces = lax.all_to_all(partial, "dp", 0, 0, tiled=True)
    piece = shape((rank, share), F32)
    grad_in, grad_out, up_out, up_back = call(
        functools.partial(sum_kernel, rank), [piece, piece, half, half], pieces, up_out, up_back, out_specs=[PLAIN] * 4
    )
    return (y[0][None], up_out[None], g[0][None], up_back[None], grad_in.T[None], grad_out[None])


def solution(mesh):
    return jax.shard_map(
        body,
        mesh=mesh,
        in_specs=(
            P("section", "dp", None),
            P("section", None, "dp"),
            P("section", "dp", None),
            P("section", "dp", None),
            P("section", "dp", None),
            P("section", "dp", None),
            P("section", None, "dp", None),
            P("section", None, "dp", None),
            P(None, None, "dp", None),
        ),
        out_specs=(
            P("section", "dp", None),
            P("section", "dp", None),
            P("section", "dp", None),
            P("section", "dp", None),
            P("section", "dp", None),
            P("section", None, "dp"),
        ),
        check_vma=False,
    )
```

time: 179 us -> 175 us (0.978)
  waiting for transfers between devices: 86.5 us -> 66.5 us
  starting transfers between devices: 68.9 us -> 81.3 us
  local copies, waits for them, and re-layouts: 6.67 us -> 9.13 us
    ppermute x1, waiting for transfers between devices: 44.6 us -> 0.01 us  [body(): xu = lax.ppermute(up_state[0], 'section', mirror)]
    all_to_all x1, waiting for transfers between devices: 0.01 us -> 24.5 us  [body(): lax.all_to_all(jnp.broadcast_to(shard[None], (replicas,) + shard.shape),...]
    all_to_all x1, waiting for transfers between devices: 6.28 us -> 14.7 us  [body(): pieces = lax.all_to_all(partial, 'dp', 0, 0, tiled=True)]
    ppermute x7 -> x8, starting transfers between devices: 31.7 us -> 38.1 us  [the longest x2 18.7 us: body(): x = (lax.ppermute(y[0], 'section', higher),)]
    ppermute x7 -> x8, waiting for transfers between devices: 33.3 us -> 27.3 us  [the longest x2 12.6 us: body(): c = (lax.ppermute(g[0], 'section', lower),)]
    ppermute x1, starting transfers between devices: 2.91 us -> 6.88 us  [body(): xu = lax.ppermute(up_state[0], 'section', mirror)]
    squeeze x0 -> x2, local copies, waits for them, and re-layouts: none -> 3.56 us  [the longest x1 1.89 us: body(): later = lax.ppermute(up_stash[0, 1:], 'section', mirror)]
    ppermute x1, waiting for transfers between devices: 2.3 us -> 0.01 us  [body(): cu = lax.ppermute(up_cot[0], 'section', mirror)]
  transfers between devices with their start and end apart: 11 -> 12, of which waited for: 7 -> 8; matrix products, arithmetic and copies ran while one was open for 1% -> 2% of each run, Pallas kernels for 5% -> 6%
where the time goes in v2:
time: 175 us; the launch traced here: 174 us
  starting transfers between devices  81.3 us (46%)
  waiting for transfers between devices  66.5 us (38%)
  Pallas kernels  15.1 us (9%)
  local copies, waits for them, and re-layouts  9.13 us (5%)
    all_to_all x1, waiting for transfers between devices, body(): lax.all_to_all(jnp.broadcast_to(shard[None], (replicas,) + shard.shape),...  24.5 us
    all_to_all x1, starting transfers between devices, body(): pieces = lax.all_to_all(partial, 'dp', 0, 0, tiled=True)  20.5 us
    ppermute x2, starting transfers between devices, body(): x = (lax.ppermute(y[0], 'section', higher),)  18.7 us
    pallas_call x8, Pallas kernels, call(): pl.pallas_call(kernel, out_shape=out, in_specs=specs, out_specs=jax.tree....  15.1 us
    all_to_all x1, waiting for transfers between devices, body(): pieces = lax.all_to_all(partial, 'dp', 0, 0, tiled=True)  14.7 us
    ppermute x2, waiting for transfers between devices, body(): c = (lax.ppermute(g[0], 'section', lower),)  12.6 us
    all_to_all x1, starting transfers between devices, body(): lax.all_to_all(jnp.broadcast_to(shard[None], (replicas,) + shard.shape),...  8.73 us
    ppermute x1, starting transfers between devices, body(): up_out = lax.ppermute(y[1], 'section', mirror)  7.86 us
  transfers between devices with their start and end apart: 12, of which 8 were waited for; matrix products, arithmetic and copies ran while one was open for 2% of the time, Pallas kernels for 6%

profile of v2, /device:TPU:135, one launch (start us, length us, event | category | flops | bytes accessed | tf_op | source)
XLA Modules:
  0.0 173.8 jit_solution(13664346497763306396)
XLA Ops:
  1.5 1.5 broadcast_in_dim.36
  3.1 8.7 %all-to-all-start = ((bf16[16,128,512]{2,1,0:T(8,128)(2,1)}), bf16[16,128,512]{2,1,0:T(8,128)(2,1)S(1)}, u32[]{:S(2)}, u32[]{:S(2)}) async-start(bf16[16,128,512]{2,1,0:T(8,128)(2,1)} %broadcast_in_dim.36), calls=%async_computation | async-start | bytes 4194304 | tf_op jit(solution)/shard_map/all_to_all | solution.py:192
  11.8 6.9 %collective-permute-start = (bf16[16,8192]{1,0:T(8,128)(2,1)}, bf16[16,8192]{1,0:T(8,128)(2,1)}, u32[]{:S(2)}, u32[]{:S(2)}) collective-permute-start(bf16[16,8192]{1,0:T(8,128)(2,1)} %bitcast.3), channel_id=1, source_target_pairs={{0,496},{16,480},{32,464},{48,448},{64,432},{80,416},{96,400},{112... | collective-permute-start | bytes 786440 | tf_op jit(solution)/shard_map/ppermute | solution.py:185
  18.7 1.7 slice_bitcast_fusion.3
  20.4 2.9 %collective-permute-start.3 = (bf16[16,8192]{1,0:T(8,128)(2,1)}, bf16[16,8192]{1,0:T(8,128)(2,1)}, u32[]{:S(2)}, u32[]{:S(2)}) collective-permute-start(bf16[16,8192]{1,0:T(8,128)(2,1)} %slice_bitcast_fusion.3), channel_id=1, source_target_pairs={{0,496},{16,480},{32,464},{48,448},{64,432},{80,416},{96,400},{112... | collective-permute-start | bytes 786440 | tf_op jit(solution)/shard_map/ppermute | solution.py:184
  23.3 7.0 %collective-permute-start.5 = (bf16[16,8192]{1,0:T(8,128)(2,1)}, bf16[16,8192]{1,0:T(8,128)(2,1)}, u32[]{:S(2)}, u32[]{:S(2)}) collective-permute-start(bf16[16,8192]{1,0:T(8,128)(2,1)} %bitcast.16), channel_id=1, source_target_pairs={{0,496},{16,480},{32,464},{48,448},{64,432},{80,416},{96,400},{112... | collective-permute-start | bytes 786440 | tf_op jit(solution)/shard_map/ppermute | solution.py:186
  30.3 1.9 %slice_bitcast_fusion = bf16[2,16,8192]{2,1,0:T(8,128)(2,1)} fusion(bf16[1,3,16,8192]{3,2,1,0:T(8,128)(2,1)} %param.16), kind=kLoop, calls=%fused_computation | loop fusion | bytes 1048576 | tf_op jit(solution)/shard_map/squeeze | solution.py:187
  32.2 2.9 %collective-permute-start.4 = (bf16[2,16,8192]{2,1,0:T(8,128)(2,1)}, bf16[2,16,8192]{2,1,0:T(8,128)(2,1)S(1)}, u32[]{:S(2)}, u32[]{:S(2)}) collective-permute-start(bf16[2,16,8192]{2,1,0:T(8,128)(2,1)} %slice_bitcast_fusion), channel_id=1, source_target_pairs={{0,496},{16,480},{32,464},{48,448},{64,432},{80,416},{96,400},{112... | collective-permute-start | bytes 1572872 | tf_op jit(solution)/shard_map/ppermute | solution.py:187
  35.2 24.5 %all-to-all-done.refs_2_.refs_5_.refs_3_.refs_4_ = bf16[16,128,512]{2,1,0:T(8,128)(2,1)S(1)} async-done(((bf16[16,128,512]{2,1,0:T(8,128)(2,1)}), bf16[16,128,512]{2,1,0:T(8,128)(2,1)S(1)}, u32[]{:S(2)}, u32[]{:S(2)}) %all-to-all-start) | async-done | bytes 2097184 | tf_op jit(solution)/shard_map/all_to_all | solution.py:192
  59.7 0.9 copy-done.2
  60.6 1.9 %shard_map.136.refs_2_.refs_8_ = bf16[32,8192]{1,0:T(8,128)(2,1)S(1)} custom-call(s32[2]{0:T(128)S(1)} %add_convert_fusion.flags, bf16[16,8192]{1,0:T(8,128)(2,1)S(1)} %bitcast.38, bf16[1,16,8192]{2,1,0:T(8,128)(2,1)} %bitcast.4.refs_1_, bf16[16,128,512]{2,1,0:T(8,128)(2,1)S(1)} %all-to-all-done.refs_2_.refs_5_.refs_3_.refs_4_), custom_call_target="tpu_custom_call" | custom-call | flops 67108864 | bytes 3145736 | tf_op jit(solution)/shard_map/pallas_call | solution.py:159
  62.6 10.1 %collective-permute-start.1 = (bf16[32,8192]{1,0:T(8,128)(2,1)S(1)}, bf16[32,8192]{1,0:T(8,128)(2,1)S(1)}, u32[]{:S(2)}, u32[]{:S(2)}) collective-permute-start(bf16[32,8192]{1,0:T(8,128)(2,1)S(1)} %shard_map.136.refs_2_.refs_8_), channel_id=1, source_target_pairs={{0,16},{16,32},{32,48},{48,64},{64,80},{80,96},{96,112},{112,128},... | collective-permute-start | bytes 1572872 | tf_op jit(solution)/shard_map/ppermute | solution.py:224
  72.7 2.4 %shard_map.139 = (bf16[32,64]{1,0:T(8,128)(2,1)S(1)}, bf16[32,64]{1,0:T(8,128)(2,1)S(1)}, bf16[32,8192]{1,0:T(8,128)(2,1)S(1)}) custom-call(s32[2]{0:T(128)S(1)} %add_convert_fusion.flags, bf16[3,16,8192]{2,1,0:T(8,128)(2,1)S(1)} %bitcast.34, bf16[1,16,8192]{2,1,0:T(8,128)(2,1)} %bitcast.13.su_ref.first_ref, bf16[16,8192]{1,0:T(8,128)(2,1)S(1)} %bitcast.39, ...), custom_call_target="tpu_custom_call" | custom-call | flops 100663296 | bytes 5251080 | tf_op jit(solution)/shard_map/pallas_call | solution.py:159
  75.1 1.9 %collective-permute-start.6 = (bf16[32,8192]{1,0:T(8,128)(2,1)S(1)}, bf16[32,8192]{1,0:T(8,128)(2,1)S(1)}, u32[]{:S(2)}, u32[]{:S(2)}) collective-permute-start(bf16[32,8192]{1,0:T(8,128)(2,1)S(1)} %get-tuple-element.23), channel_id=1, source_target_pairs={{16,0},{32,16},{48,32},{64,48},{80,64},{96,80},{112,96},{128,112},... | collective-permute-start | bytes 1572872 | tf_op jit(solution)/shard_map/ppermute | solution.py:225
  77.1 3.8 %collective-permute-done.1.refs_0_.refs_4_ = bf16[32,8192]{1,0:T(8,128)(2,1)S(1)} collective-permute-done((bf16[32,8192]{1,0:T(8,128)(2,1)S(1)}, bf16[32,8192]{1,0:T(8,128)(2,1)S(1)}, u32[]{:S(2)}, u32[]{:S(2)}) %collective-permute-start.1) | collective-permute-done | bytes 524320 | tf_op jit(solution)/shard_map/ppermute | solution.py:224
  80.8 1.5 shard_map.137.refs_1_.refs_9_
  82.3 8.7 %collective-permute-start.2 = (bf16[32,8192]{1,0:T(8,128)(2,1)S(1)}, bf16[32,8192]{1,0:T(8,128)(2,1)S(1)}, u32[]{:S(2)}, u32[]{:S(2)}) collective-permute-start(bf16[32,8192]{1,0:T(8,128)(2,1)S(1)} %shard_map.137.refs_1_.refs_9_), channel_id=1, source_target_pairs={{0,16},{16,32},{32,48},{48,64},{64,80},{80,96},{96,112},{112,128},... | collective-permute-start | bytes 1572872 | tf_op jit(solution)/shard_map/ppermute | solution.py:224
  91.0 2.2 %collective-permute-done.6.refs_2_.refs_6_ = bf16[32,8192]{1,0:T(8,128)(2,1)S(1)} collective-permute-done((bf16[32,8192]{1,0:T(8,128)(2,1)S(1)}, bf16[32,8192]{1,0:T(8,128)(2,1)S(1)}, u32[]{:S(2)}, u32[]{:S(2)}) %collective-permute-start.6) | collective-permute-done | bytes 524320 | tf_op jit(solution)/shard_map/ppermute | solution.py:225
  93.2 1.7 shard_map.140
  94.9 1.9 %collective-permute-start.7 = (bf16[32,8192]{1,0:T(8,128)(2,1)S(1)}, bf16[32,8192]{1,0:T(8,128)(2,1)S(1)}, u32[]{:S(2)}, u32[]{:S(2)}) collective-permute-start(bf16[32,8192]{1,0:T(8,128)(2,1)S(1)} %get-tuple-element.24), channel_id=1, source_target_pairs={{16,0},{32,16},{48,32},{64,48},{80,64},{96,80},{112,96},{128,112},... | collective-permute-start | bytes 1572872 | tf_op jit(solution)/shard_map/ppermute | solution.py:225
  97.1 2.2 %shard_map.138 = (bf16[16,8192]{1,0:T(8,128)(2,1)}, bf16[16,8192]{1,0:T(8,128)(2,1)S(1)}) custom-call(s32[2]{0:T(128)S(1)} %add_convert_fusion.flags, bf16[32,8192]{1,0:T(8,128)(2,1)S(1)} %collective-permute-done.2.refs_0_.refs_5_, bf16[2,16,8192]{2,1,0:T(8,128)(2,1)S(1)} %get-tuple-element.38.refs_1_, ...), custom_call_target="tpu_custom_call" | custom-call | flops 67108864 | bytes 3670024 | tf_op jit(solution)/shard_map/pallas_call | solution.py:159
  99.3 10.4 %collective-permute-done.7.refs_3_.refs_7_ = bf16[32,8192]{1,0:T(8,128)(2,1)S(1)} collective-permute-done((bf16[32,8192]{1,0:T(8,128)(2,1)S(1)}, bf16[32,8192]{1,0:T(8,128)(2,1)S(1)}, u32[]{:S(2)}, u32[]{:S(2)}) %collective-permute-start.7) | collective-permute-done | bytes 524320 | tf_op jit(solution)/shard_map/ppermute | solution.py:225
  110.6 2.4 %shard_map.141 = (bf16[32,64]{1,0:T(8,128)(2,1)S(1)}, bf16[32,64]{1,0:T(8,128)(2,1)S(1)}, bf16[16,8192]{1,0:T(8,128)(2,1)}, bf16[16,8192]{1,0:T(8,128)(2,1)S(1)}) custom-call(s32[2]{0:T(128)S(1)} %add_convert_fusion.flags, bf16[3,16,8192]{2,1,0:T(8,128)(2,1)S(1)} %bitcast.36, bf16[2,16,8192]{2,1,0:T(8,128)(2,1)S(1)} %collective-permute-done.4.su_ref.later_ref, ...), custom_call_target="tpu_custom_call" | custom-call | flops 100663296 | bytes 5513224 | tf_op jit(solution)/shard_map/pallas_call | solution.py:159
  113.7 1.9 %shard_map.142 = bf16[16,128,512]{2,1,0:T(8,128)(2,1)S(1)} custom-call(s32[2]{0:T(128)S(1)} %add_convert_fusion.flags, bf16[3,16,8192]{2,1,0:T(8,128)(2,1)S(1)} %bitcast.37, bf16[1,16,8192]{2,1,0:T(8,128)(2,1)} %bitcast.13.su_ref.first_ref, bf16[2,16,8192]{2,1,0:T(8,128)(2,1)S(1)} %collective-permute-done.4.su_ref.later_ref, bf16[16,8192]{1,0:T(8,128)(2,1)S(1)} %bitcast.40, ...), custom_call_target="tpu_custom_call" | custom-call | flops 201326592 | bytes 8413192 | tf_op jit(solution)/shard_map/pallas_call | solution.py:159
  115.6 1.3 copy-done.1
  117.0 20.5 %all-to-all-start.1 = ((bf16[16,128,512]{2,1,0:T(8,128)(2,1)}), bf16[16,128,512]{2,1,0:T(8,128)(2,1)S(1)}, u32[]{:S(2)}, u32[]{:S(2)}) async-start(bf16[16,128,512]{2,1,0:T(8,128)(2,1)} %copy-done.1), calls=%async_computation.1 | async-start | bytes 4194304 | tf_op jit(solution)/shard_map/all_to_all | solution.py:234
  137.5 1.9 %collective-permute-start.9 = (bf16[16,8192]{1,0:T(8,128)(2,1)S(1)}, bf16[16,8192]{1,0:T(8,128)(2,1)S(1)}, u32[]{:S(2)}, u32[]{:S(2)}) collective-permute-start(bf16[16,8192]{1,0:T(8,128)(2,1)S(1)} %copy-done.8), channel_id=1, source_target_pairs={{0,496},{16,480},{32,464},{48,448},{64,432},{80,416},{96,400},{112... | collective-permute-start | bytes 786440 | tf_op jit(solution)/shard_map/ppermute | solution.py:233
  139.4 7.9 %collective-permute-start.8 = (bf16[16,8192]{1,0:T(8,128)(2,1)S(1)}, bf16[16,8192]{1,0:T(8,128)(2,1)S(1)}, u32[]{:S(2)}, u32[]{:S(2)}) collective-permute-start(bf16[16,8192]{1,0:T(8,128)(2,1)S(1)} %copy-done.6), channel_id=1, source_target_pairs={{0,496},{16,480},{32,464},{48,448},{64,432},{80,416},{96,400},{112... | collective-permute-start | bytes 786440 | tf_op jit(solution)/shard_map/ppermute | solution.py:232
  147.3 4.0 %collective-permute-done.9.g_ref = bf16[16,8192]{1,0:T(8,128)(2,1)S(1)} collective-permute-done((bf16[16,8192]{1,0:T(8,128)(2,1)S(1)}, bf16[16,8192]{1,0:T(8,128)(2,1)S(1)}, u32[]{:S(2)}, u32[]{:S(2)}) %collective-permute-start.9) | collective-permute-done | bytes 262176 | tf_op jit(solution)/shard_map/ppermute | solution.py:233
  151.3 6.7 %collective-permute-done.8.y_ref = bf16[16,8192]{1,0:T(8,128)(2,1)S(1)} collective-permute-done((bf16[16,8192]{1,0:T(8,128)(2,1)S(1)}, bf16[16,8192]{1,0:T(8,128)(2,1)S(1)}, u32[]{:S(2)}, u32[]{:S(2)}) %collective-permute-start.8) | collective-permute-done | bytes 262176 | tf_op jit(solution)/shard_map/ppermute | solution.py:232
  158.0 14.7 %all-to-all-done.1.in_ref = bf16[16,128,512]{2,1,0:T(8,128)(2,1)S(1)} async-done(((bf16[16,128,512]{2,1,0:T(8,128)(2,1)}), bf16[16,128,512]{2,1,0:T(8,128)(2,1)S(1)}, u32[]{:S(2)}, u32[]{:S(2)}) %all-to-all-start.1) | async-done | bytes 2097184 | tf_op jit(solution)/shard_map/all_to_all | solution.py:234
  172.7 1.1 shard_map.143
  (26 shorter events, 2.9 us)
Async XLA Ops:
  3.1 56.6 %all-to-all-start = ((bf16[16,128,512]{2,1,0:T(8,128)(2,1)}), bf16[16,128,512]{2,1,0:T(8,128)(2,1)S(1)}, u32[]{:S(2)}, u32[]{:S(2)}) async-start(bf16[16,128,512]{2,1,0:T(8,128)(2,1)} %broadcast_in_dim.36), calls=%async_computation | async-start | bytes 4194304 | tf_op jit(solution)/shard_map/all_to_all | solution.py:192
  11.8 23.4 %collective-permute-start = (bf16[16,8192]{1,0:T(8,128)(2,1)}, bf16[16,8192]{1,0:T(8,128)(2,1)}, u32[]{:S(2)}, u32[]{:S(2)}) collective-permute-start(bf16[16,8192]{1,0:T(8,128)(2,1)} %bitcast.3), channel_id=1, source_target_pairs={{0,496},{16,480},{32,464},{48,448},{64,432},{80,416},{96,400},{112... | collective-permute-start | bytes 786440 | tf_op jit(solution)/shard_map/ppermute | solution.py:185
  20.4 52.3 %collective-permute-start.3 = (bf16[16,8192]{1,0:T(8,128)(2,1)}, bf16[16,8192]{1,0:T(8,128)(2,1)}, u32[]{:S(2)}, u32[]{:S(2)}) collective-permute-start(bf16[16,8192]{1,0:T(8,128)(2,1)} %slice_bitcast_fusion.3), channel_id=1, source_target_pairs={{0,496},{16,480},{32,464},{48,448},{64,432},{80,416},{96,400},{112... | collective-permute-start | bytes 786440 | tf_op jit(solution)/shard_map/ppermute | solution.py:184
  23.3 49.4 %copy-start = (bf16[1,3,16,8192]{3,2,1,0:T(8,128)(2,1)S(1)}, bf16[1,3,16,8192]{3,2,1,0:T(8,128)(2,1)}, u32[]{:S(2)}) copy-start(bf16[1,3,16,8192]{3,2,1,0:T(8,128)(2,1)} %param.15) | copy-start | bytes 2359300
  23.3 49.4 %collective-permute-start.5 = (bf16[16,8192]{1,0:T(8,128)(2,1)}, bf16[16,8192]{1,0:T(8,128)(2,1)}, u32[]{:S(2)}, u32[]{:S(2)}) collective-permute-start(bf16[16,8192]{1,0:T(8,128)(2,1)} %bitcast.16), channel_id=1, source_target_pairs={{0,496},{16,480},{32,464},{48,448},{64,432},{80,416},{96,400},{112... | collective-permute-start | bytes 786440 | tf_op jit(solution)/shard_map/ppermute | solution.py:186
  32.2 58.8 %collective-permute-start.4 = (bf16[2,16,8192]{2,1,0:T(8,128)(2,1)}, bf16[2,16,8192]{2,1,0:T(8,128)(2,1)S(1)}, u32[]{:S(2)}, u32[]{:S(2)}) collective-permute-start(bf16[2,16,8192]{2,1,0:T(8,128)(2,1)} %slice_bitcast_fusion), channel_id=1, source_target_pairs={{0,496},{16,480},{32,464},{48,448},{64,432},{80,416},{96,400},{112... | collective-permute-start | bytes 1572872 | tf_op jit(solution)/shard_map/ppermute | solution.py:187
  59.7 1.0 copy-start.2
  60.6 12.0 %copy-start.3 = (bf16[1,16,8192]{2,1,0:T(8,128)(2,1)S(1)}, bf16[1,16,8192]{2,1,0:T(8,128)(2,1)}, u32[]{:S(2)}) copy-start(bf16[1,16,8192]{2,1,0:T(8,128)(2,1)} %param.13) | copy-start | bytes 786436
  62.6 18.3 %collective-permute-start.1 = (bf16[32,8192]{1,0:T(8,128)(2,1)S(1)}, bf16[32,8192]{1,0:T(8,128)(2,1)S(1)}, u32[]{:S(2)}, u32[]{:S(2)}) collective-permute-start(bf16[32,8192]{1,0:T(8,128)(2,1)S(1)} %shard_map.136.refs_2_.refs_8_), channel_id=1, source_target_pairs={{0,16},{16,32},{32,48},{48,64},{64,80},{80,96},{96,112},{112,128},... | collective-permute-start | bytes 1572872 | tf_op jit(solution)/shard_map/ppermute | solution.py:224
  72.7 4.3 %copy-start.9 = (bf16[2,2,16,8192]{3,2,1,0:T(8,128)(2,1)S(1)}, bf16[2,2,16,8192]{3,2,1,0:T(8,128)(2,1)}, u32[]{:S(2)}) copy-start(bf16[2,2,16,8192]{3,2,1,0:T(8,128)(2,1)} %param.17) | copy-start | bytes 3145732
  75.1 18.2 %collective-permute-start.6 = (bf16[32,8192]{1,0:T(8,128)(2,1)S(1)}, bf16[32,8192]{1,0:T(8,128)(2,1)S(1)}, u32[]{:S(2)}, u32[]{:S(2)}) collective-permute-start(bf16[32,8192]{1,0:T(8,128)(2,1)S(1)} %get-tuple-element.23), channel_id=1, source_target_pairs={{16,0},{32,16},{48,32},{64,48},{80,64},{96,80},{112,96},{128,112},... | collective-permute-start | bytes 1572872 | tf_op jit(solution)/shard_map/ppermute | solution.py:225
  82.3 14.8 %collective-permute-start.2 = (bf16[32,8192]{1,0:T(8,128)(2,1)S(1)}, bf16[32,8192]{1,0:T(8,128)(2,1)S(1)}, u32[]{:S(2)}, u32[]{:S(2)}) collective-permute-start(bf16[32,8192]{1,0:T(8,128)(2,1)S(1)} %shard_map.137.refs_1_.refs_9_), channel_id=1, source_target_pairs={{0,16},{16,32},{32,48},{48,64},{64,80},{80,96},{96,112},{112,128},... | collective-permute-start | bytes 1572872 | tf_op jit(solution)/shard_map/ppermute | solution.py:224
  94.9 14.7 %collective-permute-start.7 = (bf16[32,8192]{1,0:T(8,128)(2,1)S(1)}, bf16[32,8192]{1,0:T(8,128)(2,1)S(1)}, u32[]{:S(2)}, u32[]{:S(2)}) collective-permute-start(bf16[32,8192]{1,0:T(8,128)(2,1)S(1)} %get-tuple-element.24), channel_id=1, source_target_pairs={{16,0},{32,16},{48,32},{64,48},{80,64},{96,80},{112,96},{128,112},... | collective-permute-start | bytes 1572872 | tf_op jit(solution)/shard_map/ppermute | solution.py:225
  99.3 14.4 %copy-start.5 = (bf16[16,8192]{1,0:T(8,128)(2,1)}, bf16[16,8192]{1,0:T(8,128)(2,1)S(1)}, u32[]{:S(2)}) copy-start(bf16[16,8192]{1,0:T(8,128)(2,1)S(1)} %get-tuple-element.25.refs_2_.refs_11_) | copy-start | bytes 786436
  109.7 1.0 copy-start.4
  113.0 0.7 copy-start.7
  115.6 1.3 copy-start.1
  117.0 20.5 %copy-start.8 = (bf16[16,8192]{1,0:T(8,128)(2,1)S(1)}, bf16[16,8192]{1,0:T(8,128)(2,1)}, u32[]{:S(2)}) copy-start(bf16[16,8192]{1,0:T(8,128)(2,1)} %copy-done.7) | copy-start | bytes 786436
  117.0 22.5 %copy-start.6 = (bf16[16,8192]{1,0:T(8,128)(2,1)S(1)}, bf16[16,8192]{1,0:T(8,128)(2,1)}, u32[]{:S(2)}) copy-start(bf16[16,8192]{1,0:T(8,128)(2,1)} %copy-done.5) | copy-start | bytes 786436
  117.0 55.7 %all-to-all-start.1 = ((bf16[16,128,512]{2,1,0:T(8,128)(2,1)}), bf16[16,128,512]{2,1,0:T(8,128)(2,1)S(1)}, u32[]{:S(2)}, u32[]{:S(2)}) async-start(bf16[16,128,512]{2,1,0:T(8,128)(2,1)} %copy-done.1), calls=%async_computation.1 | async-start | bytes 4194304 | tf_op jit(solution)/shard_map/all_to_all | solution.py:234
  137.5 13.8 %collective-permute-start.9 = (bf16[16,8192]{1,0:T(8,128)(2,1)S(1)}, bf16[16,8192]{1,0:T(8,128)(2,1)S(1)}, u32[]{:S(2)}, u32[]{:S(2)}) collective-permute-start(bf16[16,8192]{1,0:T(8,128)(2,1)S(1)} %copy-done.8), channel_id=1, source_target_pairs={{0,496},{16,480},{32,464},{48,448},{64,432},{80,416},{96,400},{112... | collective-permute-start | bytes 786440 | tf_op jit(solution)/shard_map/ppermute | solution.py:233
  139.4 18.6 %collective-permute-start.8 = (bf16[16,8192]{1,0:T(8,128)(2,1)S(1)}, bf16[16,8192]{1,0:T(8,128)(2,1)S(1)}, u32[]{:S(2)}, u32[]{:S(2)}) collective-permute-start(bf16[16,8192]{1,0:T(8,128)(2,1)S(1)} %copy-done.6), channel_id=1, source_target_pairs={{0,496},{16,480},{32,464},{48,448},{64,432},{80,416},{96,400},{112... | collective-permute-start | bytes 786440 | tf_op jit(solution)/shard_map/ppermute | solution.py:232

commit v3 on v1

--- a/solution.py
+++ b/solution.py
@@ -29,10 +29,17 @@
     return lax.dot_general(a, b, (((0,), (0,)), ((), ())), preferred_element_type=F32)
 
 
-def both(parts, cols):
+def join_kernel(a_ref, b_ref, c_ref, out_ref, kept_ref):
+    n = a_ref.shape[0]
+    out_ref[:n] = a_ref[...]
+    out_ref[n:] = b_ref[...]
+    kept_ref[...] = c_ref[...]
+
+
+def both(parts, spot, cols):
     if len(parts) == 1:
         return parts[0][:, cols]
-    return jnp.concatenate([part[:, cols] for part in parts], axis=0)
+    return jnp.concatenate([parts[0][:, cols], parts[1][spot, :, cols]], axis=0)
 
 
 def project(take, w_ref, half, square):
@@ -53,7 +60,7 @@
 
 def forward_kernel(n_parts, flags, *refs):
     parts, rest = refs[:n_parts], refs[n_parts:]
-    if n_parts == 1:
+    if len(rest) == 3:
         enter_ref, w_ref, y_ref = rest
         first = flags[0] == 1
 
@@ -64,7 +71,7 @@
         w_ref, y_ref = rest
 
         def take(cols):
-            return both(parts, cols)
+            return both(parts, 0, cols)
 
     blocks, _, wide = w_ref.shape
     rank = w_ref.shape[1] // 2
@@ -77,7 +84,7 @@
         y_ref[:, cols] = (take(cols).astype(F32) + nn(hidden, w_ref[j, rank:, :])).astype(BF16)
 
 
-def backward_kernel(n_x, n_c, moment, flags, sd_ref, su_ref, *refs):
+def backward_kernel(n_x, n_c, moment, spot, flags, sd_ref, su_ref, *refs):
     xs, y_ref, refs = refs[:n_x], refs[n_x], refs[n_x + 1 :]
     cs, (w_ref, g_ref, pre_grad_ref, hidden_ref) = refs[:n_c], refs[n_c:]
     blocks, _, wide = w_ref.shape
@@ -85,11 +92,11 @@
     last = flags[1] == 1
 
     def rows(cols):
-        stash = jnp.concatenate([sd_ref[moment, :, cols], su_ref[moment, :, cols]], axis=0)
-        return jnp.where(last, both(xs, cols), stash)
+        stash = jnp.concatenate([sd_ref[moment, :, cols], su_ref[spot, :, cols]], axis=0)
+        return jnp.where(last, both(xs, 0, cols), stash)
 
     def cot(cols):
-        return jnp.where(last, y_ref[:, cols], both(cs, cols))
+        return jnp.where(last, y_ref[:, cols], both(cs, 0, cols))
 
     total, squares = project(rows, w_ref, 0, True)
     hidden_grad = project(cot, w_ref, 1, False)
@@ -110,9 +117,9 @@
         ).astype(BF16)
 
 
-def terms_kernel(flags, sd_ref, su_ref, *refs):
-    xd, xu, cd, cu, x1, x2, c1, c2, y0, y1, y2 = refs[:11]
-    pre_grads, hiddens, out_ref = refs[11:14], refs[14:17], refs[17]
+def terms_kernel(flags, sd_ref, first_ref, later_ref, *refs):
+    x0, cd, cu, x1, x2, c1, c2, y0, y1, y2 = refs[:10]
+    pre_grads, hiddens, out_ref = refs[10:13], refs[13:16], refs[16]
     blocks, _, wide = out_ref.shape
     rank = out_ref.shape[1] // 2
     last = flags[1] == 1
@@ -120,10 +127,14 @@
     hidden = jnp.concatenate([r[...] for r in hiddens], axis=0)
     for j in range(blocks):
         cols = pl.ds(j * wide, wide)
-        stash = jnp.concatenate([r[t, :, cols] for t in range(TICKS) for r in (sd_ref, su_ref)], axis=0)
-        x = jnp.concatenate([r[:, cols] for r in (xd, xu, x1, x2)], axis=0)
+        stash = jnp.concatenate(
+            [sd_ref[0, :, cols], first_ref[0, :, cols], sd_ref[1, :, cols], later_ref[0, :, cols]]
+            + [sd_ref[2, :, cols], later_ref[1, :, cols]],
+            axis=0,
+        )
+        x = jnp.concatenate([x0[:, cols], x1[:, cols], x2[:, cols]], axis=0)
         y = jnp.concatenate([r[:, cols] for r in (y0, y1, y2)], axis=0)
-        c = jnp.concatenate([r[:, cols] for r in (cd, cu, c1, c2)], axis=0)
+        c = jnp.concatenate([cd[:, cols], cu[0, :, cols], c1[:, cols], c2[:, cols]], axis=0)
         out_ref[j, :rank, :] = tn(pre_grad, jnp.where(last, x, stash)).astype(BF16)
         out_ref[j, rank:, :] = tn(hidden, jnp.where(last, y, c)).astype(BF16)
 
@@ -165,9 +176,12 @@
     shape = jax.ShapeDtypeStruct
 
     xd, cd, sd = down_state[0], down_cot[0], down_stash[0]
+    first = lax.ppermute(up_stash[0, 0], "section", mirror)
     xu = lax.ppermute(up_state[0], "section", mirror)
     cu = lax.ppermute(up_cot[0], "section", mirror)
-    su = lax.ppermute(up_stash[0], "section", mirror)
+    later = lax.ppermute(up_stash[0, 1:], "section", mirror)
+    su = [first[None], later, later]
+    spots = [0, 0, 1]
 
     shard = jnp.concatenate([adapter_in[0].T, adapter_out[0]], axis=0)
     weights = lax.all_to_all(
@@ -177,7 +191,9 @@
     one = 2 * 2 * rows * width * rank
     full = shape((2 * rows, width), BF16)
     low = shape((2 * rows, rank), BF16)
-    x, c = (xd, xu), (cd, cu)
+    x0, cu = call(join_kernel, [full, shape(cu.shape, BF16)], xd, xu, cu)
+    c0 = cu[None]
+    x, c = (x0,), (cd, c0)
     xs, ys, cs, pre_grads, hiddens = [], [], [], [], []
     for moment in range(TICKS):
         enter = () if moment == 0 else (entering[:, moment - 1],)
@@ -185,9 +201,9 @@
             functools.partial(forward_kernel, len(x)), full, flags, *x, *enter, weights, flops=2 * one
         )
         g, pre_grad, hidden = call(
-            functools.partial(backward_kernel, len(x), len(c), moment),
+            functools.partial(backward_kernel, len(x), len(c), moment, spots[moment]),
             [full, low, low],
-            flags, sd, su, *x, y, *c, weights,
+            flags, sd, su[moment], *x, y, *c, weights,
             flops=3 * one,
         )
         xs.append(x)
@@ -201,7 +217,7 @@
     partial = call(
         terms_kernel,
         shape((replicas, 2 * rank, share), BF16),
-        flags, sd, su, *xs[0], *cs[0], *xs[1], *xs[2], *cs[1], *cs[2], *ys, *pre_grads, *hiddens,
+        flags, sd, su[0], later, x0, cd, c0, *xs[1], *xs[2], *cs[1], *cs[2], *ys, *pre_grads, *hiddens,
         flops=6 * one,
     )
     up_out = lax.ppermute(y[rows:], "section", mirror)

time: 179 us -> 174 us (0.972)
  waiting for transfers between devices: 86.5 us -> 60 us
  starting transfers between devices: 68.9 us -> 86.6 us
  local copies, waits for them, and re-layouts: 6.67 us -> 11.7 us
    ppermute x1, waiting for transfers between devices: 44.6 us -> 0.01 us  [body(): xu = lax.ppermute(up_state[0], 'section', mirror)]
    ppermute x1, waiting for transfers between devices: 2.3 us -> 14.1 us  [body(): cu = lax.ppermute(up_cot[0], 'section', mirror)]
    ppermute x2, waiting for transfers between devices: 22.2 us -> 13.3 us  [body(): c = (lax.ppermute(g, 'section', lower),)]
    all_to_all x1, waiting for transfers between devices: 0.01 us -> 8.85 us  [body(): lax.all_to_all(jnp.broadcast_to(shard[None], (replicas,) + shard.shape),...]
    ppermute x2, starting transfers between devices: 10.4 us -> 18.7 us  [body(): x = (lax.ppermute(y, 'section', higher),)]
    all_to_all x1, starting transfers between devices: 18.6 us -> 25.6 us  [body(): pieces = lax.all_to_all(partial, 'dp', 0, 0, tiled=True)]
    ppermute x2, waiting for transfers between devices: 0.01 us -> 4.17 us  [body(): x = (lax.ppermute(y, 'section', higher),)]
    ppermute x1, starting transfers between devices: 2.91 us -> 6.88 us  [body(): xu = lax.ppermute(up_state[0], 'section', mirror)]
  transfers between devices with their start and end apart: 11 -> 12, of which waited for: 7 -> 9; matrix products, arithmetic and copies ran while one was open for 1% -> 2% of each run, Pallas kernels for 5% -> 5%
where the time goes in v3:
time: 174 us
  starting transfers between devices  86.6 us (50%)
  waiting for transfers between devices  60 us (34%)
  Pallas kernels  13.5 us (8%)
  local copies, waits for them, and re-layouts  11.7 us (7%)
    all_to_all x1, starting transfers between devices, body(): pieces = lax.all_to_all(partial, 'dp', 0, 0, tiled=True)  25.6 us
    ppermute x2, starting transfers between devices, body(): x = (lax.ppermute(y, 'section', higher),)  18.7 us
    ppermute x1, waiting for transfers between devices, body(): cu = lax.ppermute(up_cot[0], 'section', mirror)  14.1 us
    pallas_call x9, Pallas kernels, call(): pl.pallas_call(kernel, out_shape=out, in_specs=specs, out_specs=jax.tree....  13.5 us
    ppermute x2, waiting for transfers between devices, body(): c = (lax.ppermute(g, 'section', lower),)  13.3 us
    all_to_all x1, waiting for transfers between devices, body(): pieces = lax.all_to_all(partial, 'dp', 0, 0, tiled=True)  9.37 us
    all_to_all x1, starting transfers between devices, body(): lax.all_to_all(jnp.broadcast_to(shard[None], (replicas,) + shard.shape),...  8.87 us
    all_to_all x1, waiting for transfers between devices, body(): lax.all_to_all(jnp.broadcast_to(shard[None], (replicas,) + shard.shape),...  8.85 us
  transfers between devices with their start and end apart: 12, of which 9 were waited for; matrix products, arithmetic and copies ran while one was open for 2% of the time, Pallas kernels for 5%

profile of v3, /device:TPU:135, one launch (start us, length us, event | category | flops | bytes accessed | tf_op | source)
XLA Modules:
  0.0 173.6 jit_solution(15095338188663288506)
XLA Ops:
  1.5 1.5 broadcast_in_dim.30
  3.1 8.9 %all-to-all-start = ((bf16[16,128,512]{2,1,0:T(8,128)(2,1)}), bf16[16,128,512]{2,1,0:T(8,128)(2,1)S(1)}, u32[]{:S(2)}, u32[]{:S(2)}) async-start(bf16[16,128,512]{2,1,0:T(8,128)(2,1)} %broadcast_in_dim.30), calls=%async_computation | async-start | bytes 4194304 | tf_op jit(solution)/shard_map/all_to_all | solution.py:187
  11.9 6.9 %collective-permute-start = (bf16[16,8192]{1,0:T(8,128)(2,1)}, bf16[16,8192]{1,0:T(8,128)(2,1)}, u32[]{:S(2)}, u32[]{:S(2)}) collective-permute-start(bf16[16,8192]{1,0:T(8,128)(2,1)} %bitcast.3), channel_id=1, source_target_pairs={{0,496},{16,480},{32,464},{48,448},{64,432},{80,416},{96,400},{112... | collective-permute-start | bytes 786440 | tf_op jit(solution)/shard_map/ppermute | solution.py:180
  18.8 2.9 %collective-permute-start.1 = (bf16[16,8192]{1,0:T(8,128)(2,1)}, bf16[16,8192]{1,0:T(8,128)(2,1)}, u32[]{:S(2)}, u32[]{:S(2)}) collective-permute-start(bf16[16,8192]{1,0:T(8,128)(2,1)} %bitcast.4), channel_id=1, source_target_pairs={{0,496},{16,480},{32,464},{48,448},{64,432},{80,416},{96,400},{112... | collective-permute-start | bytes 786440 | tf_op jit(solution)/shard_map/ppermute | solution.py:181
  22.5 6.9 %collective-permute-start.6 = (bf16[16,8192]{1,0:T(8,128)(2,1)}, bf16[16,8192]{1,0:T(8,128)(2,1)}, u32[]{:S(2)}, u32[]{:S(2)}) collective-permute-start(bf16[16,8192]{1,0:T(8,128)(2,1)} %slice_bitcast_fusion.5), channel_id=1, source_target_pairs={{0,496},{16,480},{32,464},{48,448},{64,432},{80,416},{96,400},{112... | collective-permute-start | bytes 786440 | tf_op jit(solution)/shard_map/ppermute | solution.py:179
  30.2 3.0 %collective-permute-start.5 = (bf16[2,16,8192]{2,1,0:T(8,128)(2,1)}, bf16[2,16,8192]{2,1,0:T(8,128)(2,1)S(1)}, u32[]{:S(2)}, u32[]{:S(2)}) collective-permute-start(bf16[2,16,8192]{2,1,0:T(8,128)(2,1)} %slice_bitcast_fusion), channel_id=1, source_target_pairs={{0,496},{16,480},{32,464},{48,448},{64,432},{80,416},{96,400},{112... | collective-permute-start | bytes 1572872 | tf_op jit(solution)/shard_map/ppermute | solution.py:182
  33.3 14.1 %collective-permute-done.1.c_ref = bf16[16,8192]{1,0:T(8,128)(2,1)} collective-permute-done((bf16[16,8192]{1,0:T(8,128)(2,1)}, bf16[16,8192]{1,0:T(8,128)(2,1)}, u32[]{:S(2)}, u32[]{:S(2)}) %collective-permute-start.1) | collective-permute-done | bytes 262176 | tf_op jit(solution)/shard_map/ppermute | solution.py:181
  47.4 0.9 copy-done.12
  48.4 1.1 shard_map.136
  51.0 8.8 %all-to-all-done.refs_1_.refs_2_.refs_4_.refs_3_ = bf16[16,128,512]{2,1,0:T(8,128)(2,1)S(1)} async-done(((bf16[16,128,512]{2,1,0:T(8,128)(2,1)}), bf16[16,128,512]{2,1,0:T(8,128)(2,1)S(1)}, u32[]{:S(2)}, u32[]{:S(2)}) %all-to-all-start) | async-done | bytes 2097184 | tf_op jit(solution)/shard_map/all_to_all | solution.py:187
  59.8 1.0 copy-done.5
  60.8 1.5 shard_map.137.refs_1_.refs_7_
  62.3 10.1 %collective-permute-start.2 = (bf16[32,8192]{1,0:T(8,128)(2,1)S(1)}, bf16[32,8192]{1,0:T(8,128)(2,1)S(1)}, u32[]{:S(2)}, u32[]{:S(2)}) collective-permute-start(bf16[32,8192]{1,0:T(8,128)(2,1)S(1)} %shard_map.137.refs_1_.refs_7_), channel_id=1, source_target_pairs={{0,16},{16,32},{32,48},{48,64},{64,80},{80,96},{96,112},{112,128},... | collective-permute-start | bytes 1572872 | tf_op jit(solution)/shard_map/ppermute | solution.py:215
  72.4 2.1 %shard_map.140 = (bf16[32,8192]{1,0:T(8,128)(2,1)S(1)}, bf16[32,64]{1,0:T(8,128)(2,1)S(1)}, bf16[32,64]{1,0:T(8,128)(2,1)S(1)}) custom-call(s32[2]{0:T(128)S(1)} %add_convert_fusion.flags, bf16[3,16,8192]{2,1,0:T(8,128)(2,1)S(1)} %bitcast.35, bf16[1,16,8192]{2,1,0:T(8,128)(2,1)} %bitcast.15.su_ref.first_ref, bf16[32,8192]{1,0:T(8,128)(2,1)S(1)} %copy-done.5, ...), custom_call_target="tpu_custom_call" | custom-call | flops 100663296 | bytes 5251080 | tf_op jit(solution)/shard_map/pallas_call | solution.py:154
  74.6 1.9 %collective-permute-start.7 = (bf16[32,8192]{1,0:T(8,128)(2,1)S(1)}, bf16[32,8192]{1,0:T(8,128)(2,1)S(1)}, u32[]{:S(2)}, u32[]{:S(2)}) collective-permute-start(bf16[32,8192]{1,0:T(8,128)(2,1)S(1)} %get-tuple-element.21), channel_id=1, source_target_pairs={{16,0},{32,16},{48,32},{64,48},{80,64},{96,80},{112,96},{128,112},... | collective-permute-start | bytes 1572872 | tf_op jit(solution)/shard_map/ppermute | solution.py:216
  76.6 4.0 %collective-permute-done.2.refs_0_.refs_3_ = bf16[32,8192]{1,0:T(8,128)(2,1)S(1)} collective-permute-done((bf16[32,8192]{1,0:T(8,128)(2,1)S(1)}, bf16[32,8192]{1,0:T(8,128)(2,1)S(1)}, u32[]{:S(2)}, u32[]{:S(2)}) %collective-permute-start.2) | collective-permute-done | bytes 524320 | tf_op jit(solution)/shard_map/ppermute | solution.py:215
  80.5 1.5 shard_map.138.refs_1_.refs_8_
  82.0 8.7 %collective-permute-start.3 = (bf16[32,8192]{1,0:T(8,128)(2,1)S(1)}, bf16[32,8192]{1,0:T(8,128)(2,1)S(1)}, u32[]{:S(2)}, u32[]{:S(2)}) collective-permute-start(bf16[32,8192]{1,0:T(8,128)(2,1)S(1)} %shard_map.138.refs_1_.refs_8_), channel_id=1, source_target_pairs={{0,16},{16,32},{32,48},{48,64},{64,80},{80,96},{96,112},{112,128},... | collective-permute-start | bytes 1572872 | tf_op jit(solution)/shard_map/ppermute | solution.py:215
  90.7 2.1 %collective-permute-done.7.refs_2_.refs_5_ = bf16[32,8192]{1,0:T(8,128)(2,1)S(1)} collective-permute-done((bf16[32,8192]{1,0:T(8,128)(2,1)S(1)}, bf16[32,8192]{1,0:T(8,128)(2,1)S(1)}, u32[]{:S(2)}, u32[]{:S(2)}) %collective-permute-start.7) | collective-permute-done | bytes 524320 | tf_op jit(solution)/shard_map/ppermute | solution.py:216
  92.8 1.6 shard_map.141
  94.5 2.1 %collective-permute-start.8 = (bf16[32,8192]{1,0:T(8,128)(2,1)S(1)}, bf16[32,8192]{1,0:T(8,128)(2,1)S(1)}, u32[]{:S(2)}, u32[]{:S(2)}) collective-permute-start(bf16[32,8192]{1,0:T(8,128)(2,1)S(1)} %get-tuple-element.22), channel_id=1, source_target_pairs={{16,0},{32,16},{48,32},{64,48},{80,64},{96,80},{112,96},{128,112},... | collective-permute-start | bytes 1572872 | tf_op jit(solution)/shard_map/ppermute | solution.py:216
  96.8 1.5 shard_map.139.refs_1_.refs_9_
  98.3 11.1 %collective-permute-done.8.refs_2_.refs_6_ = bf16[32,8192]{1,0:T(8,128)(2,1)S(1)} collective-permute-done((bf16[32,8192]{1,0:T(8,128)(2,1)S(1)}, bf16[32,8192]{1,0:T(8,128)(2,1)S(1)}, u32[]{:S(2)}, u32[]{:S(2)}) %collective-permute-start.8) | collective-permute-done | bytes 524320 | tf_op jit(solution)/shard_map/ppermute | solution.py:216
  109.4 1.6 shard_map.142
  111.8 1.7 shard_map.143
  113.5 1.3 copy-done.1
  114.9 25.6 %all-to-all-start.1 = ((bf16[16,128,512]{2,1,0:T(8,128)(2,1)}), bf16[16,128,512]{2,1,0:T(8,128)(2,1)S(1)}, u32[]{:S(2)}, u32[]{:S(2)}) async-start(bf16[16,128,512]{2,1,0:T(8,128)(2,1)} %copy-done.1), calls=%async_computation.1 | async-start | bytes 4194304 | tf_op jit(solution)/shard_map/all_to_all | solution.py:225
  141.2 1.9 %collective-permute-start.9 = (bf16[16,8192]{1,0:T(8,128)(2,1)S(1)}, bf16[16,8192]{1,0:T(8,128)(2,1)S(1)}, u32[]{:S(2)}, u32[]{:S(2)}) collective-permute-start(bf16[16,8192]{1,0:T(8,128)(2,1)S(1)} %get-tuple-element.34), channel_id=1, source_target_pairs={{0,496},{16,480},{32,464},{48,448},{64,432},{80,416},{96,400},{112... | collective-permute-start | bytes 786440 | tf_op jit(solution)/shard_map/ppermute | solution.py:224
  143.9 7.8 %collective-permute-start.4 = (bf16[16,8192]{1,0:T(8,128)(2,1)S(1)}, bf16[16,8192]{1,0:T(8,128)(2,1)S(1)}, u32[]{:S(2)}, u32[]{:S(2)}) collective-permute-start(bf16[16,8192]{1,0:T(8,128)(2,1)S(1)} %get-tuple-element.36), channel_id=1, source_target_pairs={{0,496},{16,480},{32,464},{48,448},{64,432},{80,416},{96,400},{112... | collective-permute-start | bytes 786440 | tf_op jit(solution)/shard_map/ppermute | solution.py:223
  151.7 6.4 %collective-permute-done.9 = bf16[16,8192]{1,0:T(8,128)(2,1)S(1)} collective-permute-done((bf16[16,8192]{1,0:T(8,128)(2,1)S(1)}, bf16[16,8192]{1,0:T(8,128)(2,1)S(1)}, u32[]{:S(2)}, u32[]{:S(2)}) %collective-permute-start.9) | collective-permute-done | bytes 262176 | tf_op jit(solution)/shard_map/ppermute | solution.py:224
  158.1 3.8 %collective-permute-done.4 = bf16[16,8192]{1,0:T(8,128)(2,1)S(1)} collective-permute-done((bf16[16,8192]{1,0:T(8,128)(2,1)S(1)}, bf16[16,8192]{1,0:T(8,128)(2,1)S(1)}, u32[]{:S(2)}, u32[]{:S(2)}) %collective-permute-start.4) | collective-permute-done | bytes 262176 | tf_op jit(solution)/shard_map/ppermute | solution.py:223
  161.9 9.4 %all-to-all-done.1.in_ref = bf16[16,128,512]{2,1,0:T(8,128)(2,1)S(1)} async-done(((bf16[16,128,512]{2,1,0:T(8,128)(2,1)}), bf16[16,128,512]{2,1,0:T(8,128)(2,1)S(1)}, u32[]{:S(2)}, u32[]{:S(2)}) %all-to-all-start.1) | async-done | bytes 2097184 | tf_op jit(solution)/shard_map/all_to_all | solution.py:225
  (41 shorter events, 8.9 us)
Async XLA Ops:
  3.1 18.7 %copy-start.14 = (bf16[1,3,16,8192]{3,2,1,0:T(8,128)(2,1)S(1)}, bf16[1,3,16,8192]{3,2,1,0:T(8,128)(2,1)}, u32[]{:S(2)}) copy-start(bf16[1,3,16,8192]{3,2,1,0:T(8,128)(2,1)} %param.16) | copy-start | bytes 2359300
  3.1 56.7 %all-to-all-start = ((bf16[16,128,512]{2,1,0:T(8,128)(2,1)}), bf16[16,128,512]{2,1,0:T(8,128)(2,1)S(1)}, u32[]{:S(2)}, u32[]{:S(2)}) async-start(bf16[16,128,512]{2,1,0:T(8,128)(2,1)} %broadcast_in_dim.30), calls=%async_computation | async-start | bytes 4194304 | tf_op jit(solution)/shard_map/all_to_all | solution.py:187
  11.9 21.3 %collective-permute-start = (bf16[16,8192]{1,0:T(8,128)(2,1)}, bf16[16,8192]{1,0:T(8,128)(2,1)}, u32[]{:S(2)}, u32[]{:S(2)}) collective-permute-start(bf16[16,8192]{1,0:T(8,128)(2,1)} %bitcast.3), channel_id=1, source_target_pairs={{0,496},{16,480},{32,464},{48,448},{64,432},{80,416},{96,400},{112... | collective-permute-start | bytes 786440 | tf_op jit(solution)/shard_map/ppermute | solution.py:180
  18.8 28.6 %collective-permute-start.1 = (bf16[16,8192]{1,0:T(8,128)(2,1)}, bf16[16,8192]{1,0:T(8,128)(2,1)}, u32[]{:S(2)}, u32[]{:S(2)}) collective-permute-start(bf16[16,8192]{1,0:T(8,128)(2,1)} %bitcast.4), channel_id=1, source_target_pairs={{0,496},{16,480},{32,464},{48,448},{64,432},{80,416},{96,400},{112... | collective-permute-start | bytes 786440 | tf_op jit(solution)/shard_map/ppermute | solution.py:181
  22.5 49.9 %collective-permute-start.6 = (bf16[16,8192]{1,0:T(8,128)(2,1)}, bf16[16,8192]{1,0:T(8,128)(2,1)}, u32[]{:S(2)}, u32[]{:S(2)}) collective-permute-start(bf16[16,8192]{1,0:T(8,128)(2,1)} %slice_bitcast_fusion.5), channel_id=1, source_target_pairs={{0,496},{16,480},{32,464},{48,448},{64,432},{80,416},{96,400},{112... | collective-permute-start | bytes 786440 | tf_op jit(solution)/shard_map/ppermute | solution.py:179
  30.2 42.2 %copy-start = (bf16[1,3,16,8192]{3,2,1,0:T(8,128)(2,1)S(1)}, bf16[1,3,16,8192]{3,2,1,0:T(8,128)(2,1)}, u32[]{:S(2)}) copy-start(bf16[1,3,16,8192]{3,2,1,0:T(8,128)(2,1)} %param.15) | copy-start | bytes 2359300
  30.2 60.5 %collective-permute-start.5 = (bf16[2,16,8192]{2,1,0:T(8,128)(2,1)}, bf16[2,16,8192]{2,1,0:T(8,128)(2,1)S(1)}, u32[]{:S(2)}, u32[]{:S(2)}) collective-permute-start(bf16[2,16,8192]{2,1,0:T(8,128)(2,1)} %slice_bitcast_fusion), channel_id=1, source_target_pairs={{0,496},{16,480},{32,464},{48,448},{64,432},{80,416},{96,400},{112... | collective-permute-start | bytes 1572872 | tf_op jit(solution)/shard_map/ppermute | solution.py:182
  47.4 1.0 copy-start.12
  49.4 0.8 copy-start.4
  50.2 0.7 copy-start.8
  59.8 1.0 copy-start.5
  60.8 11.6 %copy-start.7 = (bf16[1,16,8192]{2,1,0:T(8,128)(2,1)S(1)}, bf16[1,16,8192]{2,1,0:T(8,128)(2,1)}, u32[]{:S(2)}) copy-start(bf16[1,16,8192]{2,1,0:T(8,128)(2,1)} %param.13) | copy-start | bytes 786436
  60.8 11.6 %copy-start.9 = (bf16[16,8192]{1,0:T(8,128)(2,1)S(1)}, bf16[16,8192]{1,0:T(8,128)(2,1)}, u32[]{:S(2)}) copy-start(bf16[16,8192]{1,0:T(8,128)(2,1)} %copy-done.8) | copy-start | bytes 786436
  62.3 18.2 %collective-permute-start.2 = (bf16[32,8192]{1,0:T(8,128)(2,1)S(1)}, bf16[32,8192]{1,0:T(8,128)(2,1)S(1)}, u32[]{:S(2)}, u32[]{:S(2)}) collective-permute-start(bf16[32,8192]{1,0:T(8,128)(2,1)S(1)} %shard_map.137.refs_1_.refs_7_), channel_id=1, source_target_pairs={{0,16},{16,32},{32,48},{48,64},{64,80},{80,96},{96,112},{112,128},... | collective-permute-start | bytes 1572872 | tf_op jit(solution)/shard_map/ppermute | solution.py:215
  72.4 4.1 %copy-start.13 = (bf16[2,2,16,8192]{3,2,1,0:T(8,128)(2,1)S(1)}, bf16[2,2,16,8192]{3,2,1,0:T(8,128)(2,1)}, u32[]{:S(2)}) copy-start(bf16[2,2,16,8192]{3,2,1,0:T(8,128)(2,1)} %param.17) | copy-start | bytes 3145732
  74.6 18.3 %collective-permute-start.7 = (bf16[32,8192]{1,0:T(8,128)(2,1)S(1)}, bf16[32,8192]{1,0:T(8,128)(2,1)S(1)}, u32[]{:S(2)}, u32[]{:S(2)}) collective-permute-start(bf16[32,8192]{1,0:T(8,128)(2,1)S(1)} %get-tuple-element.21), channel_id=1, source_target_pairs={{16,0},{32,16},{48,32},{64,48},{80,64},{96,80},{112,96},{128,112},... | collective-permute-start | bytes 1572872 | tf_op jit(solution)/shard_map/ppermute | solution.py:216
  82.0 14.8 %collective-permute-start.3 = (bf16[32,8192]{1,0:T(8,128)(2,1)S(1)}, bf16[32,8192]{1,0:T(8,128)(2,1)S(1)}, u32[]{:S(2)}, u32[]{:S(2)}) collective-permute-start(bf16[32,8192]{1,0:T(8,128)(2,1)S(1)} %shard_map.138.refs_1_.refs_8_), channel_id=1, source_target_pairs={{0,16},{16,32},{32,48},{48,64},{64,80},{80,96},{96,112},{112,128},... | collective-permute-start | bytes 1572872 | tf_op jit(solution)/shard_map/ppermute | solution.py:215
  90.7 3.8 %copy-start.2 = (bf16[2,16,8192]{2,1,0:T(8,128)(2,1)}, bf16[2,16,8192]{2,1,0:T(8,128)(2,1)S(1)}, u32[]{:S(2)}) copy-start(bf16[2,16,8192]{2,1,0:T(8,128)(2,1)S(1)} %collective-permute-done.5.su_ref.later_ref) | copy-start | bytes 1572868
  94.5 14.9 %copy-start.3 = (bf16[2,16,8192]{2,1,0:T(8,128)(2,1)S(1)}, bf16[2,16,8192]{2,1,0:T(8,128)(2,1)}, u32[]{:S(2)}) copy-start(bf16[2,16,8192]{2,1,0:T(8,128)(2,1)} %copy-done.2) | copy-start | bytes 1572868
  94.5 14.9 %collective-permute-start.8 = (bf16[32,8192]{1,0:T(8,128)(2,1)S(1)}, bf16[32,8192]{1,0:T(8,128)(2,1)S(1)}, u32[]{:S(2)}, u32[]{:S(2)}) collective-permute-start(bf16[32,8192]{1,0:T(8,128)(2,1)S(1)} %get-tuple-element.22), channel_id=1, source_target_pairs={{16,0},{32,16},{48,32},{64,48},{80,64},{96,80},{112,96},{128,112},... | collective-permute-start | bytes 1572872 | tf_op jit(solution)/shard_map/ppermute | solution.py:216
  98.2 13.6 %copy-start.6 = (bf16[32,8192]{1,0:T(8,128)(2,1)S(1)}, bf16[32,8192]{1,0:T(8,128)(2,1)}, u32[]{:S(2)}) copy-start(bf16[32,8192]{1,0:T(8,128)(2,1)} %copy-done.4) | copy-start | bytes 1572868
  111.0 0.8 copy-start.10
  113.5 1.3 copy-start.1
  114.9 25.6 %copy-start.11 = (bf16[32,8192]{1,0:T(8,128)(2,1)S(1)}, bf16[32,8192]{1,0:T(8,128)(2,1)}, u32[]{:S(2)}) copy-start(bf16[32,8192]{1,0:T(8,128)(2,1)} %copy-done.10) | copy-start | bytes 1572868
  114.9 56.4 %all-to-all-start.1 = ((bf16[16,128,512]{2,1,0:T(8,128)(2,1)}), bf16[16,128,512]{2,1,0:T(8,128)(2,1)S(1)}, u32[]{:S(2)}, u32[]{:S(2)}) async-start(bf16[16,128,512]{2,1,0:T(8,128)(2,1)} %copy-done.1), calls=%async_computation.1 | async-start | bytes 4194304 | tf_op jit(solution)/shard_map/all_to_all | solution.py:225
  141.2 16.9 %collective-permute-start.9 = (bf16[16,8192]{1,0:T(8,128)(2,1)S(1)}, bf16[16,8192]{1,0:T(8,128)(2,1)S(1)}, u32[]{:S(2)}, u32[]{:S(2)}) collective-permute-start(bf16[16,8192]{1,0:T(8,128)(2,1)S(1)} %get-tuple-element.34), channel_id=1, source_target_pairs={{0,496},{16,480},{32,464},{48,448},{64,432},{80,416},{96,400},{112... | collective-permute-start | bytes 786440 | tf_op jit(solution)/shard_map/ppermute | solution.py:224
  143.9 18.0 %collective-permute-start.4 = (bf16[16,8192]{1,0:T(8,128)(2,1)S(1)}, bf16[16,8192]{1,0:T(8,128)(2,1)S(1)}, u32[]{:S(2)}, u32[]{:S(2)}) collective-permute-start(bf16[16,8192]{1,0:T(8,128)(2,1)S(1)} %get-tuple-element.36), channel_id=1, source_target_pairs={{0,496},{16,480},{32,464},{48,448},{64,432},{80,416},{96,400},{112... | collective-permute-start | bytes 786440 | tf_op jit(solution)/shard_map/ppermute | solution.py:223

commit v4 on v2

--- a/solution.py
+++ b/solution.py
@@ -120,7 +120,7 @@
         put(g_refs, cols, g.astype(BF16))
 
 
-def terms_kernel(flags, sd_ref, first_ref, later_ref, *refs):
+def terms_kernel(flags, sd_ref, later_ref, *refs):
     xd, xu, cd, cu, x1, x2, c1, c2, y0, y1, y2_down, y2_up = refs[:12]
     pre_grads, hiddens, out_ref = refs[12:15], refs[15:18], refs[18]
     blocks, rank, wide = out_ref.shape
@@ -131,7 +131,7 @@
     for j in range(blocks):
         cols = pl.ds(j * wide, wide)
         stash = jnp.concatenate(
-            [sd_ref[0, :, cols], first_ref[0, :, cols], sd_ref[1, :, cols], later_ref[0, :, cols]]
+            [sd_ref[0, :, cols], cu[1, :, cols], sd_ref[1, :, cols], later_ref[0, :, cols]]
             + [sd_ref[2, :, cols], later_ref[1, :, cols]],
             axis=0,
         )
@@ -181,24 +181,23 @@
     shape = jax.ShapeDtypeStruct
 
     xd, cd, sd = down_state[0], down_cot[0], down_stash[0]
-    first = lax.ppermute(up_stash[0, 0], "section", mirror)
     xu = lax.ppermute(up_state[0], "section", mirror)
-    cu = lax.ppermute(up_cot[0], "section", mirror)
+    cu = lax.ppermute(jnp.stack([up_cot[0], up_stash[0, 0]]), "section", mirror)
     later = lax.ppermute(up_stash[0, 1:], "section", mirror)
-    su = [first[None], later, later]
-    spots = [0, 0, 1]
+    su = [cu, later, later]
+    spots = [1, 0, 1]
 
     shard = jnp.concatenate([adapter_in[0].T, adapter_out[0]], axis=0)
     weights = lax.all_to_all(
         jnp.broadcast_to(shard[None], (replicas,) + shard.shape), "dp", 0, 0, tiled=True
     )
 
-    x0, c0 = xu[None], cu[None]
+    x0 = xu[None]
     one = 2 * 2 * rows * width * rank
     full = shape((2 * rows, width), BF16)
     half = shape((rows, width), BF16)
     low = shape((2 * rows, rank), BF16)
-    x, c = (xd, xu[None]), (cd, cu[None])
+    x, c = (xd, xu[None]), (cd, cu)
     xs, ys, cs, pre_grads, hiddens = [], [], [], [], []
     for moment in range(TICKS):
         enter = () if moment == 0 else (entering[:, moment - 1],)
@@ -226,7 +225,7 @@
     partial = call(
         terms_kernel,
         shape((replicas, 2 * rank, share), BF16),
-        flags, sd, su[0], later, xd, x0, cd, c0, *xs[1], *xs[2], *cs[1], *cs[2], *ys[0], *ys[1], *ys[2], *pre_grads, *hiddens,
+        flags, sd, later, xd, x0, cd, cu, *xs[1], *xs[2], *cs[1], *cs[2], *ys[0], *ys[1], *ys[2], *pre_grads, *hiddens,
         flops=6 * one,
     )
     up_out = lax.ppermute(y[1], "section", mirror)

time: 175 us -> 175 us (level)
  starting transfers between devices: 81.3 us -> 78.3 us
  waiting for transfers between devices: 66.5 us -> 69.3 us
    ppermute x2 -> x1, starting transfers between devices: 9.91 us -> 3.03 us  [body(): cu = lax.ppermute(jnp.stack([up_cot[0], up_stash[0, 0]]), 'section', mirror)]
    ppermute x1, starting transfers between devices: 2.89 us -> 6.86 us  [body(): later = lax.ppermute(up_stash[0, 1:], 'section', mirror)]
    all_to_all x1, waiting for transfers between devices: 24.5 us -> 27.3 us  [body(): lax.all_to_all(jnp.broadcast_to(shard[None], (replicas,) + shard.shape),...]
    unnamed x20 -> x22, local copies, waits for them, and re-layouts: 3.96 us -> 3.96 us
  transfers between devices with their start and end apart: 12 -> 11, of which waited for: 8 -> 8; matrix products, arithmetic and copies ran while one was open for 2% -> 2% of each run, Pallas kernels for 6% -> 6%
where the time goes in v4:
time: 175 us; the launch traced here: 174 us
  starting transfers between devices  78.3 us (45%)
  waiting for transfers between devices  69.3 us (40%)
  Pallas kernels  15.2 us (9%)
  local copies, waits for them, and re-layouts  8.43 us (5%)
  other arithmetic  1.8 us (1%)
    all_to_all x1, waiting for transfers between devices, body(): lax.all_to_all(jnp.broadcast_to(shard[None], (replicas,) + shard.shape),...  27.3 us
    all_to_all x1, starting transfers between devices, body(): pieces = lax.all_to_all(partial, 'dp', 0, 0, tiled=True)  20.3 us
    ppermute x2, starting transfers between devices, body(): x = (lax.ppermute(y[0], 'section', higher),)  18.7 us
    pallas_call x8, Pallas kernels, call(): pl.pallas_call(kernel, out_shape=out, in_specs=specs, out_specs=jax.tree....  15.2 us
    all_to_all x1, waiting for transfers between devices, body(): pieces = lax.all_to_all(partial, 'dp', 0, 0, tiled=True)  14.7 us
    ppermute x2, waiting for transfers between devices, body(): c = (lax.ppermute(g[0], 'section', lower),)  13 us
    all_to_all x1, starting transfers between devices, body(): lax.all_to_all(jnp.broadcast_to(shard[None], (replicas,) + shard.shape),...  8.87 us
    ppermute x1, starting transfers between devices, body(): up_out = lax.ppermute(y[1], 'section', mirror)  7.86 us
  transfers between devices with their start and end apart: 11, of which 8 were waited for; matrix products, arithmetic and copies ran while one was open for 2% of the time, Pallas kernels for 6%

profile of v4, /device:TPU:135, one launch (start us, length us, event | category | flops | bytes accessed | tf_op | source)
XLA Modules:
  0.0 173.9 jit_solution(4623867989232058947)
XLA Ops:
  1.5 1.5 broadcast_in_dim.29
  3.1 8.9 %all-to-all-start = ((bf16[16,128,512]{2,1,0:T(8,128)(2,1)}), bf16[16,128,512]{2,1,0:T(8,128)(2,1)S(1)}, u32[]{:S(2)}, u32[]{:S(2)}) async-start(bf16[16,128,512]{2,1,0:T(8,128)(2,1)} %broadcast_in_dim.29), calls=%async_computation | async-start | bytes 4194304 | tf_op jit(solution)/shard_map/all_to_all | solution.py:191
  11.9 6.9 %collective-permute-start = (bf16[16,8192]{1,0:T(8,128)(2,1)}, bf16[16,8192]{1,0:T(8,128)(2,1)}, u32[]{:S(2)}, u32[]{:S(2)}) collective-permute-start(bf16[16,8192]{1,0:T(8,128)(2,1)} %bitcast.3), channel_id=1, source_target_pairs={{0,496},{16,480},{32,464},{48,448},{64,432},{80,416},{96,400},{112... | collective-permute-start | bytes 786440 | tf_op jit(solution)/shard_map/ppermute | solution.py:184
  18.8 1.0 slice_bitcast_fusion.3
  20.6 3.0 %collective-permute-start.4 = (bf16[2,16,8192]{2,1,0:T(8,128)(2,1)}, bf16[2,16,8192]{2,1,0:T(8,128)(2,1)}, u32[]{:S(2)}, u32[]{:S(2)}) collective-permute-start(bf16[2,16,8192]{2,1,0:T(8,128)(2,1)} %pad_maximum_fusion), channel_id=1, source_target_pairs={{0,496},{16,480},{32,464},{48,448},{64,432},{80,416},{96,400},{112... | collective-permute-start | bytes 1572872 | tf_op jit(solution)/shard_map/ppermute | solution.py:185
  23.7 1.9 %slice_bitcast_fusion = bf16[2,16,8192]{2,1,0:T(8,128)(2,1)} fusion(bf16[1,3,16,8192]{3,2,1,0:T(8,128)(2,1)} %param.16), kind=kLoop, calls=%fused_computation.1 | loop fusion | bytes 1048576 | tf_op jit(solution)/shard_map/squeeze | solution.py:186
  25.6 6.9 %collective-permute-start.3 = (bf16[2,16,8192]{2,1,0:T(8,128)(2,1)}, bf16[2,16,8192]{2,1,0:T(8,128)(2,1)S(1)}, u32[]{:S(2)}, u32[]{:S(2)}) collective-permute-start(bf16[2,16,8192]{2,1,0:T(8,128)(2,1)} %slice_bitcast_fusion), channel_id=1, source_target_pairs={{0,496},{16,480},{32,464},{48,448},{64,432},{80,416},{96,400},{112... | collective-permute-start | bytes 1572872 | tf_op jit(solution)/shard_map/ppermute | solution.py:186
  32.5 27.3 %all-to-all-done.refs_2_.refs_5_.refs_3_.refs_4_ = bf16[16,128,512]{2,1,0:T(8,128)(2,1)S(1)} async-done(((bf16[16,128,512]{2,1,0:T(8,128)(2,1)}), bf16[16,128,512]{2,1,0:T(8,128)(2,1)S(1)}, u32[]{:S(2)}, u32[]{:S(2)}) %all-to-all-start) | async-done | bytes 2097184 | tf_op jit(solution)/shard_map/all_to_all | solution.py:191
  59.8 0.9 copy-done.2
  60.8 1.9 %shard_map.136.refs_2_.refs_8_ = bf16[32,8192]{1,0:T(8,128)(2,1)S(1)} custom-call(s32[2]{0:T(128)S(1)} %add_convert_fusion.flags, bf16[16,8192]{1,0:T(8,128)(2,1)S(1)} %bitcast.35, bf16[1,16,8192]{2,1,0:T(8,128)(2,1)} %bitcast.4.refs_1_, bf16[16,128,512]{2,1,0:T(8,128)(2,1)S(1)} %all-to-all-done.refs_2_.refs_5_.refs_3_.refs_4_), custom_call_target="tpu_custom_call" | custom-call | flops 67108864 | bytes 3145736 | tf_op jit(solution)/shard_map/pallas_call | solution.py:159
  62.7 10.1 %collective-permute-start.1 = (bf16[32,8192]{1,0:T(8,128)(2,1)S(1)}, bf16[32,8192]{1,0:T(8,128)(2,1)S(1)}, u32[]{:S(2)}, u32[]{:S(2)}) collective-permute-start(bf16[32,8192]{1,0:T(8,128)(2,1)S(1)} %shard_map.136.refs_2_.refs_8_), channel_id=1, source_target_pairs={{0,16},{16,32},{32,48},{48,64},{64,80},{80,96},{96,112},{112,128},... | collective-permute-start | bytes 1572872 | tf_op jit(solution)/shard_map/ppermute | solution.py:223
  72.8 2.5 %shard_map.139 = (bf16[32,64]{1,0:T(8,128)(2,1)S(1)}, bf16[32,64]{1,0:T(8,128)(2,1)S(1)}, bf16[32,8192]{1,0:T(8,128)(2,1)S(1)}) custom-call(s32[2]{0:T(128)S(1)} %add_convert_fusion.flags, bf16[3,16,8192]{2,1,0:T(8,128)(2,1)S(1)} %bitcast.31, bf16[2,16,8192]{2,1,0:T(8,128)(2,1)} %collective-permute-done.4.su_ref.refs_4_.refs_3_, ...), custom_call_target="tpu_custom_call" | custom-call | flops 100663296 | bytes 5775368 | tf_op jit(solution)/shard_map/pallas_call | solution.py:159
  75.3 1.9 %collective-permute-start.5 = (bf16[32,8192]{1,0:T(8,128)(2,1)S(1)}, bf16[32,8192]{1,0:T(8,128)(2,1)S(1)}, u32[]{:S(2)}, u32[]{:S(2)}) collective-permute-start(bf16[32,8192]{1,0:T(8,128)(2,1)S(1)} %get-tuple-element.23), channel_id=1, source_target_pairs={{16,0},{32,16},{48,32},{64,48},{80,64},{96,80},{112,96},{128,112},... | collective-permute-start | bytes 1572872 | tf_op jit(solution)/shard_map/ppermute | solution.py:224
  77.4 3.6 %collective-permute-done.1.refs_0_.refs_4_ = bf16[32,8192]{1,0:T(8,128)(2,1)S(1)} collective-permute-done((bf16[32,8192]{1,0:T(8,128)(2,1)S(1)}, bf16[32,8192]{1,0:T(8,128)(2,1)S(1)}, u32[]{:S(2)}, u32[]{:S(2)}) %collective-permute-start.1) | collective-permute-done | bytes 524320 | tf_op jit(solution)/shard_map/ppermute | solution.py:223
  81.0 1.5 shard_map.137.refs_1_.refs_9_
  82.4 8.7 %collective-permute-start.2 = (bf16[32,8192]{1,0:T(8,128)(2,1)S(1)}, bf16[32,8192]{1,0:T(8,128)(2,1)S(1)}, u32[]{:S(2)}, u32[]{:S(2)}) collective-permute-start(bf16[32,8192]{1,0:T(8,128)(2,1)S(1)} %shard_map.137.refs_1_.refs_9_), channel_id=1, source_target_pairs={{0,16},{16,32},{32,48},{48,64},{64,80},{80,96},{96,112},{112,128},... | collective-permute-start | bytes 1572872 | tf_op jit(solution)/shard_map/ppermute | solution.py:223
  91.1 2.4 %collective-permute-done.5.refs_2_.refs_6_ = bf16[32,8192]{1,0:T(8,128)(2,1)S(1)} collective-permute-done((bf16[32,8192]{1,0:T(8,128)(2,1)S(1)}, bf16[32,8192]{1,0:T(8,128)(2,1)S(1)}, u32[]{:S(2)}, u32[]{:S(2)}) %collective-permute-start.5) | collective-permute-done | bytes 524320 | tf_op jit(solution)/shard_map/ppermute | solution.py:224
  93.5 1.7 shard_map.140
  95.2 1.9 %collective-permute-start.6 = (bf16[32,8192]{1,0:T(8,128)(2,1)S(1)}, bf16[32,8192]{1,0:T(8,128)(2,1)S(1)}, u32[]{:S(2)}, u32[]{:S(2)}) collective-permute-start(bf16[32,8192]{1,0:T(8,128)(2,1)S(1)} %get-tuple-element.24), channel_id=1, source_target_pairs={{16,0},{32,16},{48,32},{64,48},{80,64},{96,80},{112,96},{128,112},... | collective-permute-start | bytes 1572872 | tf_op jit(solution)/shard_map/ppermute | solution.py:224
  97.2 2.2 %shard_map.138 = (bf16[16,8192]{1,0:T(8,128)(2,1)}, bf16[16,8192]{1,0:T(8,128)(2,1)S(1)}) custom-call(s32[2]{0:T(128)S(1)} %add_convert_fusion.flags, bf16[32,8192]{1,0:T(8,128)(2,1)S(1)} %collective-permute-done.2.refs_0_.refs_5_, bf16[2,16,8192]{2,1,0:T(8,128)(2,1)S(1)} %get-tuple-element.38.refs_1_, ...), custom_call_target="tpu_custom_call" | custom-call | flops 67108864 | bytes 3670024 | tf_op jit(solution)/shard_map/pallas_call | solution.py:159
  99.4 10.6 %collective-permute-done.6.refs_3_.refs_7_ = bf16[32,8192]{1,0:T(8,128)(2,1)S(1)} collective-permute-done((bf16[32,8192]{1,0:T(8,128)(2,1)S(1)}, bf16[32,8192]{1,0:T(8,128)(2,1)S(1)}, u32[]{:S(2)}, u32[]{:S(2)}) %collective-permute-start.6) | collective-permute-done | bytes 524320 | tf_op jit(solution)/shard_map/ppermute | solution.py:224
  110.0 0.9 copy-done.3
  110.9 2.4 %shard_map.141 = (bf16[32,64]{1,0:T(8,128)(2,1)S(1)}, bf16[32,64]{1,0:T(8,128)(2,1)S(1)}, bf16[16,8192]{1,0:T(8,128)(2,1)}, bf16[16,8192]{1,0:T(8,128)(2,1)S(1)}) custom-call(s32[2]{0:T(128)S(1)} %add_convert_fusion.flags, bf16[3,16,8192]{2,1,0:T(8,128)(2,1)S(1)} %bitcast.33, bf16[2,16,8192]{2,1,0:T(8,128)(2,1)S(1)} %collective-permute-done.3.su_ref.later_ref, ...), custom_call_target="tpu_custom_call" | custom-call | flops 100663296 | bytes 5513224 | tf_op jit(solution)/shard_map/pallas_call | solution.py:159
  114.0 1.9 %shard_map.142 = bf16[16,128,512]{2,1,0:T(8,128)(2,1)S(1)} custom-call(s32[2]{0:T(128)S(1)} %add_convert_fusion.flags, bf16[3,16,8192]{2,1,0:T(8,128)(2,1)S(1)} %bitcast.34, bf16[2,16,8192]{2,1,0:T(8,128)(2,1)S(1)} %collective-permute-done.3.su_ref.later_ref, bf16[16,8192]{1,0:T(8,128)(2,1)S(1)} %bitcast.37, bf16[1,16,8192]{2,1,0:T(8,128)(2,1)} %bitcast.4.refs_1_, ...), custom_call_target="tpu_custom_call" | custom-call | flops 201326592 | bytes 8413192 | tf_op jit(solution)/shard_map/pallas_call | solution.py:159
  115.9 1.3 copy-done.1
  117.3 20.3 %all-to-all-start.1 = ((bf16[16,128,512]{2,1,0:T(8,128)(2,1)}), bf16[16,128,512]{2,1,0:T(8,128)(2,1)S(1)}, u32[]{:S(2)}, u32[]{:S(2)}) async-start(bf16[16,128,512]{2,1,0:T(8,128)(2,1)} %copy-done.1), calls=%async_computation.1 | async-start | bytes 4194304 | tf_op jit(solution)/shard_map/all_to_all | solution.py:233
  137.6 1.9 %collective-permute-start.8 = (bf16[16,8192]{1,0:T(8,128)(2,1)S(1)}, bf16[16,8192]{1,0:T(8,128)(2,1)S(1)}, u32[]{:S(2)}, u32[]{:S(2)}) collective-permute-start(bf16[16,8192]{1,0:T(8,128)(2,1)S(1)} %copy-done.8), channel_id=1, source_target_pairs={{0,496},{16,480},{32,464},{48,448},{64,432},{80,416},{96,400},{112... | collective-permute-start | bytes 786440 | tf_op jit(solution)/shard_map/ppermute | solution.py:232
  139.5 7.9 %collective-permute-start.7 = (bf16[16,8192]{1,0:T(8,128)(2,1)S(1)}, bf16[16,8192]{1,0:T(8,128)(2,1)S(1)}, u32[]{:S(2)}, u32[]{:S(2)}) collective-permute-start(bf16[16,8192]{1,0:T(8,128)(2,1)S(1)} %copy-done.5), channel_id=1, source_target_pairs={{0,496},{16,480},{32,464},{48,448},{64,432},{80,416},{96,400},{112... | collective-permute-start | bytes 786440 | tf_op jit(solution)/shard_map/ppermute | solution.py:231
  147.4 3.9 %collective-permute-done.8.g_ref = bf16[16,8192]{1,0:T(8,128)(2,1)S(1)} collective-permute-done((bf16[16,8192]{1,0:T(8,128)(2,1)S(1)}, bf16[16,8192]{1,0:T(8,128)(2,1)S(1)}, u32[]{:S(2)}, u32[]{:S(2)}) %collective-permute-start.8) | collective-permute-done | bytes 262176 | tf_op jit(solution)/shard_map/ppermute | solution.py:232
  151.3 6.7 %collective-permute-done.7.y_ref = bf16[16,8192]{1,0:T(8,128)(2,1)S(1)} collective-permute-done((bf16[16,8192]{1,0:T(8,128)(2,1)S(1)}, bf16[16,8192]{1,0:T(8,128)(2,1)S(1)}, u32[]{:S(2)}, u32[]{:S(2)}) %collective-permute-start.7) | collective-permute-done | bytes 262176 | tf_op jit(solution)/shard_map/ppermute | solution.py:231
  158.1 14.7 %all-to-all-done.1.in_ref = bf16[16,128,512]{2,1,0:T(8,128)(2,1)S(1)} async-done(((bf16[16,128,512]{2,1,0:T(8,128)(2,1)}), bf16[16,128,512]{2,1,0:T(8,128)(2,1)S(1)}, u32[]{:S(2)}, u32[]{:S(2)}) %all-to-all-start.1) | async-done | bytes 2097184 | tf_op jit(solution)/shard_map/all_to_all | solution.py:233
  172.8 1.1 shard_map.143
  (27 shorter events, 2.7 us)
Async XLA Ops:
  3.1 16.7 %copy-start.10 = (bf16[1,16,8192]{2,1,0:T(8,128)(2,1)S(1)}, bf16[1,16,8192]{2,1,0:T(8,128)(2,1)}, u32[]{:S(2)}) copy-start(bf16[1,16,8192]{2,1,0:T(8,128)(2,1)} %param.14) | copy-start | bytes 786436
  3.1 56.7 %all-to-all-start = ((bf16[16,128,512]{2,1,0:T(8,128)(2,1)}), bf16[16,128,512]{2,1,0:T(8,128)(2,1)S(1)}, u32[]{:S(2)}, u32[]{:S(2)}) async-start(bf16[16,128,512]{2,1,0:T(8,128)(2,1)} %broadcast_in_dim.29), calls=%async_computation | async-start | bytes 4194304 | tf_op jit(solution)/shard_map/all_to_all | solution.py:191
  11.9 20.6 %collective-permute-start = (bf16[16,8192]{1,0:T(8,128)(2,1)}, bf16[16,8192]{1,0:T(8,128)(2,1)}, u32[]{:S(2)}, u32[]{:S(2)}) collective-permute-start(bf16[16,8192]{1,0:T(8,128)(2,1)} %bitcast.3), channel_id=1, source_target_pairs={{0,496},{16,480},{32,464},{48,448},{64,432},{80,416},{96,400},{112... | collective-permute-start | bytes 786440 | tf_op jit(solution)/shard_map/ppermute | solution.py:184
  20.6 52.1 %copy-start = (bf16[1,3,16,8192]{3,2,1,0:T(8,128)(2,1)S(1)}, bf16[1,3,16,8192]{3,2,1,0:T(8,128)(2,1)}, u32[]{:S(2)}) copy-start(bf16[1,3,16,8192]{3,2,1,0:T(8,128)(2,1)} %param.15) | copy-start | bytes 2359300
  20.6 52.1 %collective-permute-start.4 = (bf16[2,16,8192]{2,1,0:T(8,128)(2,1)}, bf16[2,16,8192]{2,1,0:T(8,128)(2,1)}, u32[]{:S(2)}, u32[]{:S(2)}) collective-permute-start(bf16[2,16,8192]{2,1,0:T(8,128)(2,1)} %pad_maximum_fusion), channel_id=1, source_target_pairs={{0,496},{16,480},{32,464},{48,448},{64,432},{80,416},{96,400},{112... | collective-permute-start | bytes 1572872 | tf_op jit(solution)/shard_map/ppermute | solution.py:185
  25.6 65.5 %collective-permute-start.3 = (bf16[2,16,8192]{2,1,0:T(8,128)(2,1)}, bf16[2,16,8192]{2,1,0:T(8,128)(2,1)S(1)}, u32[]{:S(2)}, u32[]{:S(2)}) collective-permute-start(bf16[2,16,8192]{2,1,0:T(8,128)(2,1)} %slice_bitcast_fusion), channel_id=1, source_target_pairs={{0,496},{16,480},{32,464},{48,448},{64,432},{80,416},{96,400},{112... | collective-permute-start | bytes 1572872 | tf_op jit(solution)/shard_map/ppermute | solution.py:186
  59.8 1.0 copy-start.2
  60.7 12.0 %copy-start.6 = (bf16[1,16,8192]{2,1,0:T(8,128)(2,1)S(1)}, bf16[1,16,8192]{2,1,0:T(8,128)(2,1)}, u32[]{:S(2)}) copy-start(bf16[1,16,8192]{2,1,0:T(8,128)(2,1)} %param.13) | copy-start | bytes 786436
  62.7 18.3 %collective-permute-start.1 = (bf16[32,8192]{1,0:T(8,128)(2,1)S(1)}, bf16[32,8192]{1,0:T(8,128)(2,1)S(1)}, u32[]{:S(2)}, u32[]{:S(2)}) collective-permute-start(bf16[32,8192]{1,0:T(8,128)(2,1)S(1)} %shard_map.136.refs_2_.refs_8_), channel_id=1, source_target_pairs={{0,16},{16,32},{32,48},{48,64},{64,80},{80,96},{96,112},{112,128},... | collective-permute-start | bytes 1572872 | tf_op jit(solution)/shard_map/ppermute | solution.py:223
  72.8 4.5 %copy-start.9 = (bf16[2,2,16,8192]{3,2,1,0:T(8,128)(2,1)S(1)}, bf16[2,2,16,8192]{3,2,1,0:T(8,128)(2,1)}, u32[]{:S(2)}) copy-start(bf16[2,2,16,8192]{3,2,1,0:T(8,128)(2,1)} %param.17) | copy-start | bytes 3145732
  75.3 18.2 %collective-permute-start.5 = (bf16[32,8192]{1,0:T(8,128)(2,1)S(1)}, bf16[32,8192]{1,0:T(8,128)(2,1)S(1)}, u32[]{:S(2)}, u32[]{:S(2)}) collective-permute-start(bf16[32,8192]{1,0:T(8,128)(2,1)S(1)} %get-tuple-element.23), channel_id=1, source_target_pairs={{16,0},{32,16},{48,32},{64,48},{80,64},{96,80},{112,96},{128,112},... | collective-permute-start | bytes 1572872 | tf_op jit(solution)/shard_map/ppermute | solution.py:224
  82.4 14.8 %collective-permute-start.2 = (bf16[32,8192]{1,0:T(8,128)(2,1)S(1)}, bf16[32,8192]{1,0:T(8,128)(2,1)S(1)}, u32[]{:S(2)}, u32[]{:S(2)}) collective-permute-start(bf16[32,8192]{1,0:T(8,128)(2,1)S(1)} %shard_map.137.refs_1_.refs_9_), channel_id=1, source_target_pairs={{0,16},{16,32},{32,48},{48,64},{64,80},{80,96},{96,112},{112,128},... | collective-permute-start | bytes 1572872 | tf_op jit(solution)/shard_map/ppermute | solution.py:223
  95.2 14.7 %collective-permute-start.6 = (bf16[32,8192]{1,0:T(8,128)(2,1)S(1)}, bf16[32,8192]{1,0:T(8,128)(2,1)S(1)}, u32[]{:S(2)}, u32[]{:S(2)}) collective-permute-start(bf16[32,8192]{1,0:T(8,128)(2,1)S(1)} %get-tuple-element.24), channel_id=1, source_target_pairs={{16,0},{32,16},{48,32},{64,48},{80,64},{96,80},{112,96},{128,112},... | collective-permute-start | bytes 1572872 | tf_op jit(solution)/shard_map/ppermute | solution.py:224
  99.4 14.6 %copy-start.4 = (bf16[16,8192]{1,0:T(8,128)(2,1)}, bf16[16,8192]{1,0:T(8,128)(2,1)S(1)}, u32[]{:S(2)}) copy-start(bf16[16,8192]{1,0:T(8,128)(2,1)S(1)} %get-tuple-element.25.refs_2_.refs_11_) | copy-start | bytes 786436
  110.0 1.0 copy-start.3
  113.3 0.7 copy-start.7
  115.9 1.3 copy-start.1
  117.3 20.3 %copy-start.8 = (bf16[16,8192]{1,0:T(8,128)(2,1)S(1)}, bf16[16,8192]{1,0:T(8,128)(2,1)}, u32[]{:S(2)}) copy-start(bf16[16,8192]{1,0:T(8,128)(2,1)} %copy-done.7) | copy-start | bytes 786436
  117.3 22.3 %copy-start.5 = (bf16[16,8192]{1,0:T(8,128)(2,1)S(1)}, bf16[16,8192]{1,0:T(8,128)(2,1)}, u32[]{:S(2)}) copy-start(bf16[16,8192]{1,0:T(8,128)(2,1)} %copy-done.4) | copy-start | bytes 786436
  117.3 55.5 %all-to-all-start.1 = ((bf16[16,128,512]{2,1,0:T(8,128)(2,1)}), bf16[16,128,512]{2,1,0:T(8,128)(2,1)S(1)}, u32[]{:S(2)}, u32[]{:S(2)}) async-start(bf16[16,128,512]{2,1,0:T(8,128)(2,1)} %copy-done.1), calls=%async_computation.1 | async-start | bytes 4194304 | tf_op jit(solution)/shard_map/all_to_all | solution.py:233
  137.6 13.7 %collective-permute-start.8 = (bf16[16,8192]{1,0:T(8,128)(2,1)S(1)}, bf16[16,8192]{1,0:T(8,128)(2,1)S(1)}, u32[]{:S(2)}, u32[]{:S(2)}) collective-permute-start(bf16[16,8192]{1,0:T(8,128)(2,1)S(1)} %copy-done.8), channel_id=1, source_target_pairs={{0,496},{16,480},{32,464},{48,448},{64,432},{80,416},{96,400},{112... | collective-permute-start | bytes 786440 | tf_op jit(solution)/shard_map/ppermute | solution.py:232
  139.5 18.5 %collective-permute-start.7 = (bf16[16,8192]{1,0:T(8,128)(2,1)S(1)}, bf16[16,8192]{1,0:T(8,128)(2,1)S(1)}, u32[]{:S(2)}, u32[]{:S(2)}) collective-permute-start(bf16[16,8192]{1,0:T(8,128)(2,1)S(1)} %copy-done.5), channel_id=1, source_target_pairs={{0,496},{16,480},{32,464},{48,448},{64,432},{80,416},{96,400},{112... | collective-permute-start | bytes 786440 | tf_op jit(solution)/shard_map/ppermute | solution.py:231
